TPU v7x, 256 devices: a whole 4x4x8 slice. The times are simulated.
256 devices in a mesh: task: 8 (over y_lo, x), row: 32 (over z, y_hi, core).
Axes of the slice: x: 4, y: 4 (y_hi: 2, y_lo: 2; y = y_hi * 2 + y_lo), z: 8, core: 2. Of those that a mesh axis runs over, the one named last changes fastest.
Arguments:
- delta: bfloat16 [8, 14336, 4096], P('task', 'row'), may hold values from -23 to 23
- sketch: bfloat16 [8, 4096, 320], P('task'), may hold values from -6 to 6
- base: bfloat16 [14336, 4096], P('row', 'task'), may hold values from -6 to 6
Outputs:
- merged: bfloat16 [14336, 4096], P('row', 'task')
All inputs are finite; a program needn't handle non-finite values.
Results may differ from a plain program's by a relative error of at most 0.0052.
Values may be sent and summed in bfloat16 or wider, within the bound.
A program may use at most 128 MiB of HBM per device.

v0:
```python
import math

import jax
import jax.numpy as jnp
from jax import lax
from jax.sharding import PartitionSpec as P

ITERS = 2


highest = lax.Precision.HIGHEST


def right_solve(factor, matrix):
    return lax.linalg.triangular_solve(
        factor, matrix, left_side=False, lower=True, transpose_a=True
    )


def local(delta, sketch, base):
    task_count = lax.axis_size("task")
    delta_rows = delta[0]
    task_sketch = sketch[0]
    shrink = 1.0 / math.sqrt(task_count)
    sketched = jnp.dot(delta_rows, task_sketch, preferred_element_type=jnp.float32)
    square = lax.psum(jnp.dot(sketched.T, sketched, precision=highest), "row")
    factor = jnp.linalg.cholesky(square)
    basis_part = right_solve(factor, sketched) * shrink
    first_sweep = 0
    for sweep in range(first_sweep, ITERS):
        gathered_basis = lax.all_gather(basis_part, "task", axis=1, tiled=True)
        column_gram = lax.psum(jnp.dot(gathered_basis.T, basis_part, precision=highest), "row")
        basis_part = 1.5 * basis_part - 0.5 * jnp.dot(
            gathered_basis, column_gram, precision=highest
        )
    weights = basis_part.astype(jnp.bfloat16)
    summed = lax.psum_scatter(
        lax.dot_general(
            delta_rows, weights, (((0,), (0,)), ((), ())), preferred_element_type=jnp.float32
        ),
        "row",
        scatter_dimension=0,
        tiled=True,
    )
    rounded = summed.astype(jnp.bfloat16)
    complete = lax.all_gather(rounded, "row", axis=0, tiled=True)
    row_block = lax.all_to_all(complete, "task", split_axis=0, concat_axis=1, tiled=True)
    all_weights = lax.all_gather(weights, "task", axis=1, tiled=True)
    update = lax.dot_general(
        all_weights, row_block, (((1,), (1,)), ((), ())), preferred_element_type=jnp.float32
    )
    return (base.astype(jnp.float32) + update).astype(jnp.bfloat16)


def solution(mesh):
    return jax.shard_map(
        local,
        mesh=mesh,
        in_specs=(P("task", "row", None), P("task", None, None), P("row", "task")),
        out_specs=P("row", "task"),
        check_vma=False,
    )
```

profile of v0, /device:TPU:1, one launch (start us, length us, event | category | flops | bytes accessed | tf_op | source)
XLA Modules:
  0.0 1446.0 jit_solution(2229295242572089464)
XLA Ops:
  6.5 1.7 copy-done
  8.3 3.6 fusion.1
  11.8 2.0 fusion.31
  13.8 0.3 all-gather.5.cloned.1.call-start
  14.2 267.6 %all-reduce.7.cloned.1.call-done = f32[320,320]{0,1:T(8,128)} async-done(((f32[320,320]{0,1:T(8,128)}), f32[320,320]{0,1:T(8,128)}) %all-reduce.7.cloned.1.call-update) | async-done | bytes 409616 | tf_op jit(solution)/shard_map/psum | solution.py:26
  281.8 2.0 copy.16
  283.8 1.2 fusion.8
  285.1 0.8 copy-done.7
  285.9 11.7 cholesky.78
  297.6 10.4 custom-call.22
  308.0 0.8 cholesky.174
  308.8 1.8 constant_dynamic-update-slice_fusion.2
  310.7 1.2 convolution_subtract_fusion.2
  311.8 0.6 cholesky.202
  312.4 12.5 cholesky.164
  325.0 0.7 select_reduce_fusion
  325.7 11.1 custom-call.23
  336.8 0.8 convolution_dynamic-update-slice_fusion
  337.6 1.1 convolution_subtract_fusion.3
  338.8 5.8 cholesky.186
  344.6 0.6 select_reduce_fusion.2
  345.2 0.7 compare_reduce_fusion
  345.9 0.7 compare_reduce_fusion.1
  348.4 1.1 select_select_fusion
  349.5 0.1 triangular_solve.94
  349.6 0.7 copy-done.6
  350.3 6.9 while.1
  350.3 0.6 fusion.50
  350.9 2.8 bitcast_dynamic-update-slice_fusion.2
  353.7 0.6 fusion.50
  354.3 2.8 bitcast_dynamic-update-slice_fusion.2
  357.2 0.1 fusion.20
  357.2 0.9 pad_maximum_fusion.1
  358.2 30.1 %custom-call.24 = f32[3,128,128]{1,2,0:T(8,128)} custom-call(f32[3,128,128]{2,1,0:T(8,128)S(1)} %pad_maximum_fusion.1), custom_call_target="InvertDiagBlocksLowerTriangular" | custom-call | tf_op jit(solution)/shard_map/triangular_solve | solution.py:15
  388.3 1.4 fusion.13
  389.7 1.3 convolution_subtract_fusion
  391.0 1.4 fusion.18
  392.4 1.5 convolution_subtract_fusion.1
  393.9 1.3 fusion.25
  395.2 0.9 fusion.9
  396.2 2.2 copy.19
  398.5 66.4 %all-gather.5.cloned.1.call-done = f32[448,2560]{0,1:T(8,128)} async-done(((f32[448,320]{0,1:T(8,128)}), f32[448,2560]{0,1:T(8,128)}) %all-gather.5.cloned.1.call-update) | async-done | bytes 4587536 | tf_op jit(solution)/shard_map/all_gather | solution.py:31
  464.8 8.9 fusion.28
  473.8 0.2 all-gather.7.cloned.1.call-start
  474.0 273.4 %all-reduce.9.cloned.1.call-done = f32[2560,320]{0,1:T(8,128)} async-done(((f32[2560,320]{0,1:T(8,128)}), f32[2560,320]{0,1:T(8,128)}) %all-reduce.9.cloned.1.call-update) | async-done | bytes 3276816 | tf_op jit(solution)/shard_map/psum | solution.py:32
  747.4 19.1 %fusion.5 = f32[448,320]{1,0:T(8,128)S(1)} fusion(f32[448,2560]{0,1:T(8,128)} %all-gather.5.cloned.1.call-done, f32[2560,320]{0,1:T(8,128)} %all-reduce.9.cloned.1.call-done, f32[448,64]{1,0:T(8,128)} %copy-done.5, f32[448,128]{1,0:T(8,128)} %copy-done.1, f32[448,128]{1,0:T(8,128)S(1)} %fusion.13), kind=kOutput, calls=%fused_computation.12 | convolution fusion | flops 4404736000 | bytes 9011200 | tf_op jit(solution)/shard_map/dot_general | solution.py:33
  766.6 1.1 copy.21
  767.8 0.0 all-reduce.11.cloned.1.call-start
  767.8 68.2 %all-gather.7.cloned.1.call-done = f32[448,2560]{0,1:T(8,128)} async-done(((f32[448,320]{0,1:T(8,128)}), f32[448,2560]{0,1:T(8,128)}) %all-gather.7.cloned.1.call-update) | async-done | bytes 4587536 | tf_op jit(solution)/shard_map/all_gather | solution.py:31
  836.0 8.8 fusion.32
  844.8 0.3 reduce-scatter.2.cloned.1.call-start
  845.1 273.3 %all-reduce.11.cloned.1.call-done = f32[2560,320]{0,1:T(8,128)} async-done(((f32[2560,320]{0,1:T(8,128)}), f32[2560,320]{0,1:T(8,128)}) %all-reduce.11.cloned.1.call-update) | async-done | bytes 3276816 | tf_op jit(solution)/shard_map/psum | solution.py:32
  1118.4 19.2 %fusion.7 = bf16[448,320]{1,0:T(8,128)(2,1)S(1)} fusion(f32[448,2560]{0,1:T(8,128)} %all-gather.7.cloned.1.call-done, f32[2560,320]{0,1:T(8,128)} %all-reduce.11.cloned.1.call-done, f32[448,320]{1,0:T(8,128)S(1)} %fusion.5), kind=kOutput, calls=%fused_computation.14 | convolution fusion | flops 4404592640 | bytes 8724480 | tf_op jit(solution)/shard_map/dot_general | solution.py:33
  1137.6 0.7 copy-done.2
  1138.3 3.9 convolution_bitcast_fusion
  1142.3 0.0 all-gather.11.cloned.1.call-start
  1142.3 131.3 %reduce-scatter.2.cloned.1.call-done = f32[128,320]{0,1:T(8,128)} async-done(((f32[4096,320]{0,1:T(8,128)}), f32[128,320]{0,1:T(8,128)}) %reduce-scatter.2.cloned.1.call-update) | async-done | bytes 163856 | tf_op jit(solution)/shard_map/reduce_scatter | solution.py:37
  1273.7 1.6 convert_element_type.14
  1275.3 0.9 copy.23
  1276.2 82.6 %all-gather.11.cloned.1.call-done = bf16[4096,320]{0,1:T(8,128)(2,1)} async-done(((bf16[128,320]{0,1:T(8,128)(2,1)}), bf16[4096,320]{0,1:T(8,128)(2,1)}) %all-gather.11.cloned.1.call-update) | async-done | bytes 2621456 | tf_op jit(solution)/shard_map/all_gather | solution.py:46
  1358.8 3.5 copy.32
  1362.3 4.6 all-to-all-start
  1366.8 67.4 %all-gather.9.cloned.1.call-done = bf16[448,2560]{0,1:T(8,128)(2,1)} async-done(((bf16[448,320]{0,1:T(8,128)(2,1)}), bf16[448,2560]{0,1:T(8,128)(2,1)}) %all-gather.9.cloned.1.call-update) | async-done | bytes 2293776 | tf_op jit(solution)/shard_map/all_gather | solution.py:48
  1434.3 4.7 fusion.4
  (35 shorter events, 0.3 us)
Async XLA Ops:
  6.5 1.7 copy-start
  6.5 275.3 %all-reduce.7.cloned.1.call-start = ((), (), s32[]{:S(2)}) async-start(), calls=%async_computation.2 | async-start | bytes 983040 | tf_op jit(solution)/shard_map/psum | solution.py:26
  13.8 451.0 %all-gather.5.cloned.1.call-start = ((), (), s32[]{:S(2)}) async-start(), calls=%async_computation.3 | async-start | bytes 5898240 | tf_op jit(solution)/shard_map/all_gather | solution.py:31
  285.1 0.8 copy-start.7
  349.5 0.8 copy-start.6
  392.4 2.8 copy-start.1
  395.2 78.5 %copy-start.5 = (f32[448,64]{1,0:T(8,128)}, f32[448,64]{1,0:T(8,128)S(1)}, u32[]{:S(2)}) copy-start(f32[448,64]{1,0:T(8,128)S(1)} %fusion.25) | copy-start | bytes 344068
  398.4 349.0 %all-reduce.9.cloned.1.call-start = ((), (), s32[]{:S(2)}) async-start(), calls=%async_computation.4 | async-start | bytes 6553600 | tf_op jit(solution)/shard_map/psum | solution.py:32
  473.8 362.2 %all-gather.7.cloned.1.call-start = ((), (), s32[]{:S(2)}) async-start(), calls=%async_computation.5 | async-start | bytes 5898240 | tf_op jit(solution)/shard_map/all_gather | solution.py:31
  767.8 350.6 %all-reduce.11.cloned.1.call-start = ((), (), s32[]{:S(2)}) async-start(), calls=%async_computation.6 | async-start | bytes 6553600 | tf_op jit(solution)/shard_map/psum | solution.py:32
  844.8 428.9 %reduce-scatter.2.cloned.1.call-start = ((), (), s32[]{:S(2)}) async-start(), calls=%async_computation.8 | async-start | bytes 5406720 | tf_op jit(solution)/shard_map/reduce_scatter | solution.py:37
  1118.4 20.0 %copy-start.4 = (bf16[1,448,4096]{2,1,0:T(8,128)(2,1)S(1)}, bf16[1,448,4096]{2,1,0:T(8,128)(2,1)}, u32[]{:S(2)}) copy-start(bf16[1,448,4096]{2,1,0:T(8,128)(2,1)} %param.3) | copy-start | bytes 11010052
  1137.6 0.7 copy-start.2
  1142.2 133.0 %copy-start.3 = (bf16[448,320]{1,0:T(8,128)(2,1)S(1)}, bf16[448,320]{1,0:T(8,128)(2,1)}, u32[]{:S(2)}) copy-start(bf16[448,320]{1,0:T(8,128)(2,1)} %copy-done.2) | copy-start | bytes 860164
  1142.3 216.5 %all-gather.11.cloned.1.call-start = ((), (), s32[]{:S(2)}) async-start(), calls=%async_computation.9 | async-start | bytes 2703360 | tf_op jit(solution)/shard_map/all_gather | solution.py:46
  1275.2 159.1 %all-gather.9.cloned.1.call-start = ((), (), s32[]{:S(2)}) async-start(), calls=%async_computation.7 | async-start | bytes 2949120 | tf_op jit(solution)/shard_map/all_gather | solution.py:48
  1362.3 72.0 %copy-start.8 = (bf16[448,512]{1,0:T(8,128)(2,1)S(1)}, bf16[448,512]{1,0:T(8,128)(2,1)}, u32[]{:S(2)}) copy-start(bf16[448,512]{1,0:T(8,128)(2,1)} %param.5) | copy-start | bytes 1376260
  1362.3 72.0 %all-to-all-start = ((bf16[8,512,320]{1,2,0:T(8,128)(2,1)}), bf16[8,512,320]{1,2,0:T(8,128)(2,1)}, u32[]{:S(2)}, u32[]{:S(2)}) async-start(bf16[8,512,320]{1,2,0:T(8,128)(2,1)} %bitcast.70), calls=%async_computation.1 | async-start | bytes 5242880 | tf_op jit(solution)/shard_map/all_to_all | solution.py:47
Sparse Core Ops, SparseCore 0:
  14.0 267.7 all-reduce.6
  398.5 66.2 all-gather.4
  473.9 273.5 all-reduce.8
  767.9 68.0 all-gather.6
  844.9 273.4 all-reduce.10
  1142.4 131.2 reduce-scatter.1
  1276.5 82.2 all-gather.10
  1360.7 73.5 all-gather.8
where the time goes:
time: 1450 us
  waiting for transfers between devices  1230 us (85%)
  other arithmetic  90.3 us (6%)
  matrix products  81.9 us (6%)
  local copies, waits for them, and re-layouts  22.1 us (2%)
  between operations  15.8 us (1%)
    psum x2, waiting for transfers between devices, local(): lax.psum(jnp.dot(gathered_basis.T, basis_part, precision=highest), 'row')  547 us
    psum x1, waiting for transfers between devices, local(): square = lax.psum(jnp.dot(sketched.T, sketched, precision=highest), 'row')  268 us
    all_gather x2, waiting for transfers between devices, local(): gathered_basis = lax.all_gather(basis_part, 'task', axis=1, tiled=True)  135 us
    reduce_scatter x1, waiting for transfers between devices, local(): lax.psum_scatter(lax.dot_general(delta_rows, weights, (((0,), (0,)), ((),...  131 us
    all_gather x1, waiting for transfers between devices, local(): complete = lax.all_gather(rounded, 'row', axis=0, tiled=True)  82.6 us
    all_gather x1, waiting for transfers between devices, local(): all_weights = lax.all_gather(weights, 'task', axis=1, tiled=True)  67.4 us
    another operation x10, other arithmetic, local(): factor = jnp.linalg.cholesky(square)  54.3 us
    dot_general x2, matrix products, local(): jnp.dot(gathered_basis, column_gram, precision=highest)  38.4 us
  transfers between devices with their start and end apart: 9, of which 8 were waited for; matrix products, arithmetic and copies ran while one was open for 0% of the time, Pallas kernels for 0%

commit v1 on v0

v1 whole, which is shorter than its diff:
```python
import functools
import math

import jax
import jax.numpy as jnp
from jax import lax
from jax.experimental import pallas as pl
from jax.experimental.pallas import tpu as pltpu
from jax.sharding import PartitionSpec as P

highest = lax.Precision.HIGHEST
MESH = pl.DeviceIdType.MESH
VMEM = pl.BlockSpec(memory_space=pltpu.VMEM)
DMA = pltpu.SemaphoreType.DMA
f32 = jnp.float32
bf16 = jnp.bfloat16
CB = 64


def params(cid):
    return pltpu.CompilerParams(
        collective_id=cid, has_side_effects=True, vmem_limit_bytes=48 * 1024 * 1024
    )


def place(chips):
    row = lax.axis_index("row")
    chip, core = row // 2, row % 2
    return chip, core, chip * 2 + (1 - core)


def around(me, step, count):
    return (me + step) % count


def remote(src, dst, ssem, rsem, where):
    return pltpu.make_async_remote_copy(
        src_ref=src, dst_ref=dst, send_sem=ssem, recv_sem=rsem,
        device_id=where, device_id_type=MESH,
    )


def loop(lo, hi, body):
    def step(i, carry):
        body(i)
        return carry

    lax.fori_loop(lo, hi, step, 0)


def greet(chips, tasks, rows):
    barrier = pltpu.get_barrier_semaphore()
    total = 0
    if rows:
        chip, core, sib = place(chips)
        pl.semaphore_signal(barrier, inc=1, device_id={"row": sib}, device_id_type=MESH)
        loop(1, chips, lambda d: pl.semaphore_signal(
            barrier, inc=1, device_id={"row": around(chip, d, chips) * 2 + core},
            device_id_type=MESH))
        total += chips
    if tasks:
        me = lax.axis_index("task")
        loop(1, tasks, lambda d: pl.semaphore_signal(
            barrier, inc=1, device_id={"task": around(me, d, tasks)}, device_id_type=MESH))
        total += tasks - 1
    pl.semaphore_wait(barrier, total)


def to_chips(chips, src, dst, ssem, rsem):
    chip, core, _ = place(chips)

    def body(d):
        other = around(chip, d, chips)
        remote(src(other), dst(d), ssem.at[d], rsem.at[d], {"row": other * 2 + core}).start()

    loop(1, chips, body)


def wait_chips(chips, src, dst, ssem, rsem):
    chip, core, _ = place(chips)

    def body(d):
        other = around(chip, d, chips)
        copy = remote(src(other), dst(d), ssem.at[d], rsem.at[d], {"row": other * 2 + core})
        copy.wait()

    loop(1, chips, body)


def reduce_rows(chips, mine, sib_buf, half, slots, sems, parts_half, part_slot):
    raise NotImplementedError


def square_kernel(chips, in_ref, out_ref, sib_buf, half, slots, core_s, core_r, a_s, a_r, b_s, b_r):
    chip, core, sib = place(chips)
    greet(chips, 0, True)
    swap = remote(in_ref.at[1 - core], sib_buf, core_s.at[0], core_r.at[0], {"row": sib})
    swap.start()
    swap.wait()
    half[...] = in_ref[core] + sib_buf[...]
    src, dst = (lambda c: half.at[c]), (lambda d: slots.at[d])
    to_chips(chips, src, dst, a_s, a_r)
    wait_chips(chips, src, dst, a_s, a_r)
    total = lax.fori_loop(1, chips, lambda d, t: t + slots[d], half[chip])
    out_ref[core, chip] = total
    src = lambda c: out_ref.at[core, chip]
    to_chips(chips, src, lambda d: out_ref.at[core, chip], b_s, b_r)
    wait_chips(chips, src, lambda d: out_ref.at[core, around(chip, chips - d, chips)], b_s, b_r)
    swap = remote(out_ref.at[core], out_ref.at[core], core_s.at[1], core_r.at[1], {"row": sib})
    swap.start()
    swap.wait_send()
    remote(out_ref.at[core], out_ref.at[1 - core], core_s.at[1], core_r.at[1], {"row": sib}).wait_recv()


def all_reduce_square(packed, chips):
    rows, lanes = packed.shape
    part = rows // (2 * chips)
    shaped = packed.reshape(2, chips, part, lanes)
    out = pl.pallas_call(
        functools.partial(square_kernel, chips),
        out_shape=jax.ShapeDtypeStruct(shaped.shape, f32),
        in_specs=[VMEM],
        out_specs=VMEM,
        scratch_shapes=[pltpu.VMEM((chips, part, lanes), f32)] * 3
        + [DMA((2,)), DMA((2,))] + [DMA((chips,))] * 4,
        compiler_params=params(1),
        name="square_sum",
    )(shaped)
    return out.reshape(rows, lanes)


def dot_nt(a, b):
    return lax.dot_general(a, b, (((1,), (1,)), ((), ())), precision=highest,
                           preferred_element_type=f32)


def dot_nn(a, b):
    return lax.dot_general(a, b, (((1,), (0,)), ((), ())), precision=highest,
                           preferred_element_type=f32)


def chol_kernel(blocks, a_ref, z_ref, cols, fac, inv):
    row_id = lax.broadcasted_iota(jnp.int32, (CB, 2 * CB), 0)
    lane_id = lax.broadcasted_iota(jnp.int32, (CB, 2 * CB), 1)
    eye = (lane_id == row_id + CB).astype(f32)
    inv[...] = jnp.zeros_like(inv)
    cols[...] = a_ref[...]
    for k in range(blocks):
        at = k * CB
        both = jnp.concatenate([cols[k, at:at + CB, :], jnp.zeros((CB, CB), f32)], axis=1) + eye
        for j in range(CB):
            scale = lax.rsqrt(both[j:j + 1, j:j + 1])
            line = both[j:j + 1, :] * scale
            down = both[:, j:j + 1] * scale
            below = both - down * line
            both = jnp.where(row_id > j, below, jnp.where(row_id == j, line, both))
        zkk = both[:, CB:]
        if k + 1 < blocks:
            panel = dot_nt(cols[k, at + CB:, :], zkk)
            fac[k, at + CB:, :] = panel
            for j in range(k + 1, blocks):
                off = (j - k - 1) * CB
                cols[j, j * CB:, :] = cols[j, j * CB:, :] - dot_nt(
                    panel[off:, :], panel[off:off + CB, :])
        for c in range(k):
            acc = dot_nn(fac[c, at:at + CB, :], inv[c, c * CB:(c + 1) * CB, :])
            for m in range(c + 1, k):
                acc = acc + dot_nn(fac[m, at:at + CB, :], inv[c, m * CB:(m + 1) * CB, :])
            inv[c, at:at + CB, :] = -dot_nn(zkk, acc)
        inv[k, at:at + CB, :] = zkk
    z_ref[...] = inv[...]


def inverse_factor(square):
    n = square.shape[0]
    blocks = n // CB
    a = jnp.transpose(square.reshape(n, blocks, CB), (1, 0, 2))
    z = pl.pallas_call(
        functools.partial(chol_kernel, blocks),
        out_shape=jax.ShapeDtypeStruct((blocks, n, CB), f32),
        in_specs=[VMEM],
        out_specs=VMEM,
        scratch_shapes=[pltpu.VMEM((blocks, n, CB), f32)] * 3,
        compiler_params=pltpu.CompilerParams(vmem_limit_bytes=32 * 1024 * 1024),
        name="inverse_factor",
    )(a)
    return jnp.transpose(z, (1, 0, 2)).reshape(n, n)


def start_tasks(tasks, src, dst, ssem, rsem):
    me = lax.axis_index("task")

    def body(d):
        other = around(me, d, tasks)
        remote(src(other), dst(me), ssem.at[d], rsem.at[d], {"task": other}).start()

    loop(1, tasks, body)


def wait_tasks(tasks, src, dst, ssem, rsem):
    me = lax.axis_index("task")

    def body(d):
        other = around(me, d, tasks)
        back = around(me, tasks - d, tasks)
        remote(src(other), dst(back), ssem.at[d], rsem.at[d], {"task": other}).wait()

    loop(1, tasks, body)


def gather_kernel(tasks, in_ref, out_ref, a_s, a_r):
    me = lax.axis_index("task")
    greet(0, tasks, False)
    src, dst = (lambda c: in_ref), (lambda c: out_ref.at[c])
    start_tasks(tasks, src, dst, a_s, a_r)
    out_ref[me] = in_ref[...]
    wait_tasks(tasks, src, dst, a_s, a_r)


def gather_tasks(block, tasks):
    return pl.pallas_call(
        functools.partial(gather_kernel, tasks),
        out_shape=jax.ShapeDtypeStruct((tasks,) + block.shape, block.dtype),
        in_specs=[VMEM],
        out_specs=VMEM,
        scratch_shapes=[DMA((tasks,)), DMA((tasks,))],
        compiler_params=params(2),
        name="basis_gather",
    )(block)


def poly_kernel(chips, tasks, in_ref, out_ref, sib_buf, half, slots, column, slab, slab2, slab3,
                core_s, core_r, a_s, a_r, b_s, b_r, c_s, c_r, t1_s, t1_r, t2_s, t2_r, t3_s, t3_r):
    chip, core, sib = place(chips)
    me = lax.axis_index("task")
    greet(chips, tasks, True)
    swap = remote(in_ref.at[:, 1 - core], sib_buf, core_s.at[0], core_r.at[0], {"row": sib})
    swap.start()
    swap.wait()
    half[...] = (in_ref[:, core].astype(f32) + sib_buf[...].astype(f32)).astype(bf16)
    src, dst = (lambda c: half.at[c]), (lambda d: slots.at[d])
    to_chips(chips, src, dst, a_s, a_r)
    wait_chips(chips, src, dst, a_s, a_r)
    gram = lax.fori_loop(
        1, chips, lambda d, t: t + slots[d].astype(f32), half[chip].astype(f32))
    mine = gram.astype(bf16)
    slab[me] = mine
    column[chip, core] = mine
    tsrc = lambda c: slab.at[me]
    start_tasks(tasks, tsrc, lambda c: slab.at[c], t1_s, t1_r)
    rsrc = lambda c: column.at[chip, core]
    to_chips(chips, rsrc, lambda d: column.at[chip, core], b_s, b_r)
    wait_chips(chips, rsrc, lambda d: column.at[around(chip, chips - d, chips), core], b_s, b_r)
    swap = remote(column.at[:, core], column.at[:, core], core_s.at[1], core_r.at[1], {"row": sib})
    swap.start()
    wait_tasks(tasks, tsrc, lambda c: slab.at[c], t1_s, t1_r)
    swap.wait_send()
    remote(column.at[:, core], column.at[:, 1 - core], core_s.at[1], core_r.at[1],
           {"row": sib}).wait_recv()

    depth, width = slab.shape[1:]
    per = width // depth // 2

    def times(left):
        def body(s, total):
            block = column[pl.ds(s * per, per)].reshape(width, width)
            return total + jnp.dot(left[s], block, preferred_element_type=f32)
        return lax.fori_loop(0, tasks, body, jnp.zeros((depth, width), f32))

    two = times(slab)
    slab2[me] = two.astype(bf16)
    src2 = lambda c: slab2.at[me]
    start_tasks(tasks, src2, lambda c: slab2.at[c], t2_s, t2_r)
    wait_tasks(tasks, src2, lambda c: slab2.at[c], t2_s, t2_r)
    three = times(slab2)
    slab3[me] = three.astype(bf16)
    src3 = lambda c: slab3.at[me]
    start_tasks(tasks, src3, lambda c: slab3.at[c], t3_s, t3_r)
    wait_tasks(tasks, src3, lambda c: slab3.at[c], t3_s, t3_r)
    four = times(slab3)
    poly = -2.4375 * gram + 1.6875 * two - 0.5625 * three + 0.0625 * four
    out_ref[chip, core] = poly.astype(bf16)
    osrc = lambda c: out_ref.at[chip, core]
    to_chips(chips, osrc, lambda d: out_ref.at[chip, core], c_s, c_r)
    wait_chips(chips, osrc, lambda d: out_ref.at[around(chip, chips - d, chips), core], c_s, c_r)
    swap = remote(out_ref.at[:, core], out_ref.at[:, core], core_s.at[2], core_r.at[2], {"row": sib})
    swap.start()
    swap.wait_send()
    remote(out_ref.at[:, core], out_ref.at[:, 1 - core], core_s.at[2], core_r.at[2],
           {"row": sib}).wait_recv()


def polynomial(partial, chips, tasks):
    total, width = partial.shape
    depth = total // (2 * chips)
    shaped = partial.reshape(chips, 2, depth, width)
    out = pl.pallas_call(
        functools.partial(poly_kernel, chips, tasks),
        out_shape=jax.ShapeDtypeStruct(shaped.shape, bf16),
        in_specs=[VMEM],
        out_specs=VMEM,
        scratch_shapes=[pltpu.VMEM((chips, depth, width), bf16)] * 3
        + [pltpu.VMEM(shaped.shape, bf16)]
        + [pltpu.VMEM((tasks, depth, width), bf16)] * 3
        + [DMA((3,)), DMA((3,))] + [DMA((chips,))] * 6 + [DMA((tasks,))] * 6,
        compiler_params=params(3),
        name="polynomial",
    )(shaped)
    return out.reshape(total, width)


def coef_kernel(chips, tasks, in_ref, w_ref, out_ref, wall_ref, sib_buf, half, slots, mine, block,
                core_s, core_r, a_s, a_r, b_s, b_r, t1_s, t1_r, w_s, w_r):
    chip, core, sib = place(chips)
    me = lax.axis_index("task")
    greet(chips, tasks, True)
    swap = remote(in_ref.at[:, :, 1 - core], sib_buf, core_s.at[0], core_r.at[0], {"row": sib})
    swap.start()
    wsrc, wdst = (lambda c: w_ref), (lambda c: wall_ref.at[c])
    start_tasks(tasks, wsrc, wdst, w_s, w_r)
    wall_ref[me] = w_ref[...]
    swap.wait()

    def add(u):
        half[u] = (in_ref[u, :, core].astype(f32) + sib_buf[u].astype(f32)).astype(bf16)

    loop(0, tasks, add)
    src, dst = (lambda c: half.at[:, c]), (lambda d: slots.at[d])
    to_chips(chips, src, dst, a_s, a_r)
    wait_chips(chips, src, dst, a_s, a_r)
    total = lax.fori_loop(
        1, chips, lambda d, t: t + slots[d].astype(f32), half[:, chip].astype(f32))
    mine[...] = total.astype(bf16)
    block[me] = mine[me]
    tsrc, tdst = (lambda c: mine.at[c]), (lambda c: block.at[c])
    start_tasks(tasks, tsrc, tdst, t1_s, t1_r)
    wait_tasks(tasks, tsrc, tdst, t1_s, t1_r)
    out_ref[:, chip, core] = block[...]
    rsrc = lambda c: block
    to_chips(chips, rsrc, lambda d: out_ref.at[:, chip, core], b_s, b_r)
    wait_chips(chips, rsrc, lambda d: out_ref.at[:, around(chip, chips - d, chips), core], b_s, b_r)
    swap = remote(out_ref.at[:, :, core], out_ref.at[:, :, core], core_s.at[1], core_r.at[1],
                  {"row": sib})
    swap.start()
    wait_tasks(tasks, wsrc, wdst, w_s, w_r)
    swap.wait_send()
    remote(out_ref.at[:, :, core], out_ref.at[:, :, 1 - core], core_s.at[1], core_r.at[1],
           {"row": sib}).wait_recv()


def coefficients_and_weights(partial, weights, chips, tasks):
    features, width = partial.shape
    depth = features // (tasks * chips * 2)
    shaped = partial.reshape(tasks, chips, 2, depth, width)
    out, wall = pl.pallas_call(
        functools.partial(coef_kernel, chips, tasks),
        out_shape=(jax.ShapeDtypeStruct(shaped.shape, bf16),
                   jax.ShapeDtypeStruct((tasks,) + weights.shape, bf16)),
        in_specs=[VMEM, VMEM],
        out_specs=(VMEM, VMEM),
        scratch_shapes=[pltpu.VMEM((tasks, chips, depth, width), bf16)] * 2
        + [pltpu.VMEM((chips, tasks, depth, width), bf16)]
        + [pltpu.VMEM((tasks, depth, width), bf16)] * 2
        + [DMA((2,)), DMA((2,))] + [DMA((chips,))] * 4 + [DMA((tasks,))] * 4,
        compiler_params=params(4),
        name="coefficients",
    )(shaped, weights)
    return out.reshape(tasks, features // tasks, width), wall


def pack(square):
    n = square.shape[0]
    parts = []
    for at in range(0, n, 128):
        piece = square[at:, at:min(at + 128, n)]
        parts.append(jnp.pad(piece, ((0, 0), (0, 128 - piece.shape[1]))))
    return jnp.concatenate(parts, axis=0)


def unpack(packed, n):
    parts, top = [], 0
    for at in range(0, n, 128):
        piece = packed[top:top + n - at, :min(128, n - at)]
        parts.append(jnp.pad(piece, ((at, 0), (0, 0))))
        top += n - at
    return jnp.concatenate(parts, axis=1)


def local(delta, sketch, base):
    tasks = lax.axis_size("task")
    chips = lax.axis_size("row") // 2
    delta_rows, task_sketch = delta[0], sketch[0]
    width = task_sketch.shape[1]
    sketched = jnp.dot(delta_rows, task_sketch, preferred_element_type=f32)
    packed = pack(jnp.dot(sketched.T, sketched, precision=highest))
    unit = 16 * chips
    packed = jnp.pad(packed, ((0, -packed.shape[0] % unit), (0, 0)))
    square = unpack(all_reduce_square(packed, chips), width)
    inverse = inverse_factor(square)
    own = lax.dot_general(
        sketched, inverse, (((1,), (1,)), ((), ())), precision=highest
    ) * (1.0 / math.sqrt(tasks))
    stack = gather_tasks(own.astype(bf16), tasks)
    gram = lax.dot_general(
        stack, own.astype(bf16), (((1,), (0,)), ((), ())), preferred_element_type=f32
    ).reshape(tasks * width, width).astype(bf16)
    poly = polynomial(gram, chips, tasks).reshape(tasks, width, width)
    weights = (
        2.25 * own
        + lax.dot_general(stack, poly, (((0, 2), (0, 1)), ((), ())), preferred_element_type=f32)
    ).astype(bf16)
    partial = lax.dot_general(
        delta_rows, weights, (((0,), (0,)), ((), ())), preferred_element_type=f32
    ).astype(bf16)
    coefs, stack2 = coefficients_and_weights(partial, weights, chips, tasks)
    update = lax.dot_general(
        stack2, coefs, (((0, 2), (0, 2)), ((), ())), preferred_element_type=f32
    )
    return (base.astype(f32) + update).astype(bf16)


def solution(mesh):
    return jax.shard_map(
        local,
        mesh=mesh,
        in_specs=(P("task", "row", None), P("task", None, None), P("row", "task")),
        out_specs=P("row", "task"),
        check_vma=False,
    )
```

time: 1450 us -> 356 us (0.25)
  waiting for transfers between devices: 1230 us -> 0 us
  Pallas kernels: 0 us -> 326 us
  other arithmetic: 90.3 us -> 0.83 us
  matrix products: 81.9 us -> 17.7 us
  between operations: 15.8 us -> 0.19 us
    psum x3 -> x0, waiting for transfers between devices: 814 us -> none  [the longest x2 547 us: local(): lax.psum(jnp.dot(gathered_basis.T, basis_part, precision=highest), 'row')]
    pallas_call x0 -> x5, Pallas kernels: none -> 326 us  [the longest x1 111 us: coefficients_and_weights(): pl.pallas_call(functools.partial(coef_kernel, chips, tasks), out_shape=(j...]
    all_gather x4 -> x0, waiting for transfers between devices: 285 us -> none  [the longest x2 135 us: local(): gathered_basis = lax.all_gather(basis_part, 'task', axis=1, tiled=True)]
    reduce_scatter x1 -> x0, waiting for transfers between devices: 131 us -> none  [local(): lax.psum_scatter(lax.dot_general(delta_rows, weights, (((0,), (0,)), ((),...]
    another operation x17 -> x0, other arithmetic: 86.6 us -> none  [the longest x10 54.3 us: local(): factor = jnp.linalg.cholesky(square)]
    dot_general x7 -> x6, matrix products: 66.3 us -> 14.7 us  [the longest x1 4.28 us: local(): lax.dot_general(stack2, coefs, (((0, 2), (0, 2)), ((), ())), preferred_el...]
  transfers between devices with their start and end apart: 9 -> 0, of which waited for: 8 -> 0; matrix products, arithmetic and copies ran while one was open for 0% -> 0% of each run, Pallas kernels for 0% -> 0%
where the time goes in v1:
time: 356 us
  Pallas kernels  326 us (92%)
  matrix products  17.7 us (5%)
  local copies, waits for them, and re-layouts  11 us (3%)
    pallas_call x1, Pallas kernels, coefficients_and_weights(): pl.pallas_call(functools.partial(coef_kernel, chips, tasks), out_shape=(j...  111 us
    pallas_call x1, Pallas kernels, polynomial(): pl.pallas_call(functools.partial(poly_kernel, chips, tasks), out_shape=ja...  108 us
    pallas_call x1, Pallas kernels, gather_tasks(): pl.pallas_call(functools.partial(gather_kernel, tasks), out_shape=jax.Sha...  46.1 us
    pallas_call x1, Pallas kernels, all_reduce_square(): pl.pallas_call(functools.partial(square_kernel, chips), out_shape=jax.Sha...  31.8 us
    pallas_call x1, Pallas kernels, inverse_factor(): pl.pallas_call(functools.partial(chol_kernel, blocks), out_shape=jax.Shap...  29.8 us

profile of v1, /device:TPU:1, one launch (start us, length us, event | category | flops | bytes accessed | tf_op | source)
XLA Modules:
  0.0 355.8 jit_solution(5332520391024757582)
XLA Ops:
  0.0 0.0 copy-start
  0.0 1.7 copy-done
  1.7 3.6 %fusion.2 = f32[448,320]{0,1:T(8,128)S(1)} fusion(bf16[1,448,4096]{2,1,0:T(8,128)(2,1)} %param.3, bf16[1,4096,320]{1,2,0:T(8,128)(2,1)S(1)} %copy-done), kind=kOutput, calls=%fused_computation.3 | convolution fusion | flops 1174405120 | bytes 6864896 | tf_op jit(solution)/shard_map/dot_general | solution.py:394
  5.3 0.0 copy-start.2
  5.3 1.2 fusion.11
  6.6 0.0 copy-done.2
  6.7 31.8 %square_sum.1 = f32[2,16,24,128]{3,2,1,0:T(8,128)S(1)} custom-call(f32[2,16,24,128]{3,2,1,0:T(8,128)S(1)} %bitcast.49), custom_call_target="tpu_custom_call" | custom-call | tf_op jit(solution)/shard_map/square_sum/pallas_call | solution.py:119
  38.5 0.1 copy.37
  38.6 0.1 copy.35
  38.7 0.1 copy.36
  38.8 0.8 select_maximum_fusion
  39.6 1.3 copy.16
  41.0 29.8 %inverse_factor.1 = f32[5,320,64]{2,1,0:T(8,128)S(1)} custom-call(f32[5,320,64]{2,1,0:T(8,128)S(1)} %bitcast.45), custom_call_target="tpu_custom_call" | custom-call | tf_op jit(solution)/shard_map/inverse_factor/pallas_call | solution.py:178
  70.8 0.0 copy-start.1
  70.8 0.9 copy-done.1
  71.7 1.5 copy.17
  73.1 2.7 multiply_convert_fusion
  75.8 46.1 %basis_gather.1 = bf16[8,448,320]{2,1,0:T(8,128)(2,1)S(1)} custom-call(bf16[448,320]{1,0:T(8,128)(2,1)S(1)} %get-tuple-element.9.in_ref), custom_call_target="tpu_custom_call" | custom-call | tf_op jit(solution)/shard_map/basis_gather/pallas_call | solution.py:221
  121.9 1.6 convolution_convert_fusion.1
  123.5 107.8 %polynomial.1 = bf16[16,2,80,320]{3,2,1,0:T(8,128)(2,1)S(1)} custom-call(bf16[16,2,80,320]{3,2,1,0:T(8,128)(2,1)S(1)} %bitcast.48), custom_call_target="tpu_custom_call" | custom-call | tf_op jit(solution)/shard_map/polynomial/pallas_call | solution.py:297
  231.3 0.0 copy-start.3
  231.3 1.4 fusion.8.w_ref
  232.7 0.7 copy-done.3
  233.4 3.1 fusion
  236.5 4.6 %copy.24 = bf16[4096,320]{1,0:T(8,128)(2,1)} copy(bf16[4096,320]{0,1:T(8,128)(2,1)} %fusion) | data formatting | bytes 5242880 | tf_op jit(solution)/shard_map/convert_element_type | solution.py:414
  241.0 0.0 copy-start.4
  241.0 110.5 %coefficients.1 = (bf16[8,16,2,16,320]{4,3,2,1,0:T(8,128)(2,1)}, bf16[8,448,320]{2,1,0:T(8,128)(2,1)S(1)}) custom-call(bf16[8,16,2,16,320]{4,3,2,1,0:T(8,128)(2,1)} %bitcast.53, bf16[448,320]{1,0:T(8,128)(2,1)S(1)} %fusion.8.w_ref), custom_call_target="tpu_custom_call" | custom-call | tf_op jit(solution)/shard_map/coefficients/pallas_call | solution.py:355
  351.5 0.0 copy-done.4
  351.5 4.3 %fusion.6 = bf16[448,512]{1,0:T(8,128)(2,1)} fusion(bf16[8,448,320]{2,1,0:T(8,128)(2,1)S(1)} %get-tuple-element.7, bf16[8,512,320]{2,1,0:T(8,128)(2,1)} %bitcast.56, bf16[448,512]{1,0:T(8,128)(2,1)S(1)} %copy-done.4), kind=kOutput, calls=%fused_computation.9 | convolution fusion | flops 1175093248 | bytes 5832704 | tf_op jit(solution)/shard_map/dot_general | solution.py:416
  (8 shorter events, 0.1 us)
Async XLA Ops:
  0.0 1.7 copy-start
  5.3 1.3 copy-start.2
  70.8 0.9 copy-start.1
  231.3 2.0 copy-start.3
  241.0 110.5 %copy-start.4 = (bf16[448,512]{1,0:T(8,128)(2,1)S(1)}, bf16[448,512]{1,0:T(8,128)(2,1)}, u32[]{:S(2)}) copy-start(bf16[448,512]{1,0:T(8,128)(2,1)} %param.5) | copy-start | bytes 1376260

commit v2 on v1

--- a/solution.py
+++ b/solution.py
@@ -87,8 +87,159 @@
     loop(1, chips, body)
 
 
-def reduce_rows(chips, mine, sib_buf, half, slots, sems, parts_half, part_slot):
-    raise NotImplementedError
+def tiles(depth, width):
+    full = width // 128
+    top = -(-depth // 32) * 16 if width % 128 else 0
+    return full, top, full * depth + top
+
+
+def pack_rows(value):
+    depth, width = value.shape
+    full, top, _ = tiles(depth, width)
+    parts = [value[:, i * 128:(i + 1) * 128] for i in range(full)]
+    if top:
+        tail = value[:, full * 128:]
+        low = jnp.concatenate(
+            [tail[top:], jnp.zeros((2 * top - depth, 64), value.dtype)], axis=0
+        ) if 2 * top > depth else tail[top:]
+        parts.append(jnp.concatenate([tail[:top], low], axis=1))
+    return jnp.concatenate(parts, axis=0)
+
+
+def unpack_rows(packed, depth, width):
+    full, top, _ = tiles(depth, width)
+    parts = [packed[i * depth:(i + 1) * depth] for i in range(full)]
+    if top:
+        tail = packed[full * depth:full * depth + top]
+        parts.append(jnp.concatenate([tail[:, :64], tail[:depth - top, 64:]], axis=0))
+    return jnp.concatenate(parts, axis=1)
+
+
+def unpack_to(dst, packed, depth, width):
+    full, top, _ = tiles(depth, width)
+    for i in range(full):
+        dst[:, i * 128:(i + 1) * 128] = packed[i * depth:(i + 1) * depth]
+    if top:
+        tail = packed[full * depth:full * depth + top]
+        dst[:top, full * 128:] = tail[:, :64]
+        dst[top:, full * 128:] = tail[:depth - top, 64:]
+
+
+def greet_near(chips, tasks):
+    barrier = pltpu.get_barrier_semaphore()
+    chip, core, sib = place(chips)
+    zs, z, y = chips // 2, chip // 2, chip % 2
+    for there in (sib, line(zs, z + 1, y, core), line(zs, z - 1, y, core), line(zs, z, 1 - y, core)):
+        pl.semaphore_signal(barrier, inc=1, device_id={"row": there}, device_id_type=MESH)
+    me = lax.axis_index("task")
+    loop(1, tasks, lambda d: pl.semaphore_signal(
+        barrier, inc=1, device_id={"task": around(me, d, tasks)}, device_id_type=MESH))
+    pl.semaphore_wait(barrier, 4 + tasks - 1)
+
+
+def line(zs, z, y, core):
+    return (((z + zs) % zs) * 2 + y) * 2 + core
+
+
+def streams(zs, y):
+    far, near = zs // 2, zs // 2 - 1
+    return [(2, 1, near, 1 - y), (3, -1, far, 1 - y), (0, 1, far, y), (1, -1, near, y)]
+
+
+def ring_reduce(chips, half, slots, other, other_in, ssem, rsem, ysem):
+    chip, core, _ = place(chips)
+    zs, z, y = chips // 2, chip // 2, chip % 2
+    hops = zs // 2
+    sent = []
+
+    def term(zz, yy):
+        return half[((zz + zs) % zs) * 2 + yy]
+
+    def send(stream, step, src):
+        k, way = stream[0], stream[1]
+        n = k * hops + step - 1
+        copy = remote(src, slots.at[n], ssem.at[n], rsem.at[n], {"row": line(zs, z + way, y, core)})
+        copy.start()
+        sent.append(copy)
+
+    def arrive(stream, step):
+        n = stream[0] * hops + step - 1
+        remote(slots.at[n], slots.at[n], ssem.at[n], rsem.at[n], {"row": line(zs, z, y, core)}).wait_recv()
+        return n
+
+    for st in streams(zs, y):
+        if st[2]:
+            dest = ((z + st[1] * st[2] + zs) % zs) * 2 + st[3]
+            send(st, 1, half.at[dest])
+    for step in range(1, hops + 1):
+        for st in streams(zs, y):
+            if step <= st[2]:
+                n = arrive(st, step)
+                if step < st[2]:
+                    dest = z + st[1] * (st[2] - step)
+                    slots[n] = (slots[n].astype(f32) + term(dest, st[3]).astype(f32)).astype(bf16)
+                    send(st, step + 1, slots.at[n])
+
+    def final(plane, pair):
+        total = term(z, plane).astype(f32)
+        for k, n in pair:
+            if n:
+                total = total + slots[k * hops + n - 1].astype(f32)
+        return total
+
+    other[...] = final(1 - y, [(2, hops - 1), (3, hops)]).astype(bf16)
+    swap = remote(other, other_in, ysem.at[0], ysem.at[1], {"row": line(zs, z, 1 - y, core)})
+    swap.start()
+    own = final(y, [(0, hops), (1, hops - 1)])
+    swap.wait()
+    for copy in sent:
+        copy.wait_send()
+    return own + other_in[...].astype(f32)
+
+
+def ring_gather(chips, at, ssem, rsem, ysem):
+    chip, core, _ = place(chips)
+    zs, z, y = chips // 2, chip // 2, chip % 2
+    hops = zs // 2
+    sent = []
+
+    def spot(zz, yy):
+        return at(((zz + zs) % zs) * 2 + yy)
+
+    def send(stream, step):
+        k, way, _, yy = stream
+        n = k * hops + step - 1
+        block = spot(z - way * (step - 1), yy)
+        copy = remote(block, block, ssem.at[n], rsem.at[n], {"row": line(zs, z + way, y, core)})
+        copy.start()
+        sent.append(copy)
+
+    def arrive(stream, step):
+        k, way, _, yy = stream
+        n = k * hops + step - 1
+        block = spot(z - way * step, yy)
+        remote(block, block, ssem.at[n], rsem.at[n], {"row": line(zs, z, y, core)}).wait_recv()
+
+    across = {"row": line(zs, z, 1 - y, core)}
+    swap = remote(spot(z, y), spot(z, y), ysem.at[2], ysem.at[3], across)
+    swap.start()
+    order = streams(zs, y)[2:] + streams(zs, y)[:2]
+    for st in order[:2]:
+        if st[2]:
+            send(st, 1)
+    remote(spot(z, 1 - y), spot(z, 1 - y), ysem.at[2], ysem.at[3], across).wait_recv()
+    for st in order[2:]:
+        if st[2]:
+            send(st, 1)
+    for step in range(1, hops + 1):
+        for st in order:
+            if step <= st[2]:
+                arrive(st, step)
+                if step < st[2]:
+                    send(st, step + 1)
+    swap.wait_send()
+    for copy in sent:
+        copy.wait_send()
 
 
 def square_kernel(chips, in_ref, out_ref, sib_buf, half, slots, core_s, core_r, a_s, a_r, b_s, b_r):
@@ -208,36 +359,93 @@
     loop(1, tasks, body)
 
 
-def gather_kernel(tasks, in_ref, out_ref, a_s, a_r):
+def spread(tasks, at, ssem, rsem):
     me = lax.axis_index("task")
+    xs = tasks // 2
+    x, y = me % xs, me // xs
+    sent = []
+
+    def send(n, block, to):
+        copy = remote(block, block, ssem.at[n], rsem.at[n], {"task": to})
+        copy.start()
+        sent.append(copy)
+
+    def arrive(n, block):
+        remote(block, block, ssem.at[n], rsem.at[n], {"task": me}).wait_recv()
+
+    def name(xx, yy):
+        return yy * xs + xx % xs
+
+    own = at(me)
+    send(0, own, name(x, 1 - y))
+    for d in range(1, xs):
+        send(d, own, name(x + d, y))
+    yield
+    twin = at(name(x, 1 - y))
+    arrive(0, twin)
+    yield name(x, 1 - y)
+    across = [d for d in range(1, xs) if d == xs // 2]
+    along = [d for d in range(1, xs) if d != xs // 2]
+    for d in along:
+        send(xs + d, twin, name(x + d, y))
+    for d in across:
+        block = at(name(x + xs - d, y))
+        arrive(d, block)
+        send(xs + d, block, name(x, 1 - y))
+        yield name(x + xs - d, y)
+    for d in along:
+        block = name(x + xs - d, y)
+        arrive(d, at(block))
+        yield block
+    for d in along + across:
+        block = name(x + xs - d, 1 - y)
+        arrive(xs + d, at(block))
+        yield block
+    for copy in sent:
+        copy.wait_send()
+
+
+def gather_kernel(tasks, in_ref, out_ref, packed, a_s, a_r):
+    me = lax.axis_index("task")
+    depth, width = in_ref.shape
     greet(0, tasks, False)
-    src, dst = (lambda c: in_ref), (lambda c: out_ref.at[c])
-    start_tasks(tasks, src, dst, a_s, a_r)
+    packed[me] = pack_rows(in_ref[...])
+    steps = spread(tasks, lambda c: packed.at[c], a_s, a_r)
+    next(steps)
     out_ref[me] = in_ref[...]
-    wait_tasks(tasks, src, dst, a_s, a_r)
+    for got in steps:
+        unpack_to(out_ref.at[got], packed[got], depth, width)
 
 
 def gather_tasks(block, tasks):
+    rows = tiles(*block.shape)[2]
     return pl.pallas_call(
         functools.partial(gather_kernel, tasks),
         out_shape=jax.ShapeDtypeStruct((tasks,) + block.shape, block.dtype),
         in_specs=[VMEM],
         out_specs=VMEM,
-        scratch_shapes=[DMA((tasks,)), DMA((tasks,))],
+        scratch_shapes=[pltpu.VMEM((tasks, rows, 128), block.dtype), DMA((tasks,)), DMA((tasks,))],
         compiler_params=params(2),
         name="basis_gather",
     )(block)
 
 
-def poly_kernel(chips, tasks, in_ref, out_ref, sib_buf, half, slots, column, slab, slab2, slab3,
+def poly_kernel(chips, tasks, in_ref, out_ref, sib_buf, half, slots, column, matrix, final, slab, slab2, slab3,
                 core_s, core_r, a_s, a_r, b_s, b_r, c_s, c_r, t1_s, t1_r, t2_s, t2_r, t3_s, t3_r):
     chip, core, sib = place(chips)
     me = lax.axis_index("task")
+    depth, width = in_ref.shape[2:]
+    per = width // depth
     greet(chips, tasks, True)
     swap = remote(in_ref.at[:, 1 - core], sib_buf, core_s.at[0], core_r.at[0], {"row": sib})
     swap.start()
     swap.wait()
-    half[...] = (in_ref[:, core].astype(f32) + sib_buf[...].astype(f32)).astype(bf16)
+
+    def add(c):
+        both = in_ref[c, core].astype(f32) + sib_buf[c].astype(f32)
+        half[c] = pack_rows(both).astype(bf16)
+
+    loop(0, chips, add)
     src, dst = (lambda c: half.at[c]), (lambda d: slots.at[d])
     to_chips(chips, src, dst, a_s, a_r)
     wait_chips(chips, src, dst, a_s, a_r)
@@ -248,60 +456,62 @@
     column[chip, core] = mine
     tsrc = lambda c: slab.at[me]
     start_tasks(tasks, tsrc, lambda c: slab.at[c], t1_s, t1_r)
-    rsrc = lambda c: column.at[chip, core]
-    to_chips(chips, rsrc, lambda d: column.at[chip, core], b_s, b_r)
-    wait_chips(chips, rsrc, lambda d: column.at[around(chip, chips - d, chips), core], b_s, b_r)
-    swap = remote(column.at[:, core], column.at[:, core], core_s.at[1], core_r.at[1], {"row": sib})
-    swap.start()
+
+    def gather(buf, sems, recvs, n):
+        block = lambda c: buf.at[chip, core]
+        to_chips(chips, block, lambda d: buf.at[chip, core], sems, recvs)
+        wait_chips(chips, block, lambda d: buf.at[around(chip, chips - d, chips), core], sems, recvs)
+        swap = remote(buf.at[:, core], buf.at[:, core], core_s.at[n], core_r.at[n], {"row": sib})
+        swap.start()
+        swap.wait_send()
+        remote(buf.at[:, core], buf.at[:, 1 - core], core_s.at[n], core_r.at[n],
+               {"row": sib}).wait_recv()
+
+    gather(column, b_s, b_r, 1)
+    loop(0, chips * 2, lambda i: unpack_to(
+        matrix.at[i], column[i // 2, i % 2], depth, width))
     wait_tasks(tasks, tsrc, lambda c: slab.at[c], t1_s, t1_r)
-    swap.wait_send()
-    remote(column.at[:, core], column.at[:, 1 - core], core_s.at[1], core_r.at[1],
-           {"row": sib}).wait_recv()
-
-    depth, width = slab.shape[1:]
-    per = width // depth // 2
 
     def times(left):
         def body(s, total):
-            block = column[pl.ds(s * per, per)].reshape(width, width)
-            return total + jnp.dot(left[s], block, preferred_element_type=f32)
+            block = matrix[pl.ds(s * per, per)].reshape(width, width)
+            return total + jnp.dot(
+                unpack_rows(left[s], depth, width), block, preferred_element_type=f32)
         return lax.fori_loop(0, tasks, body, jnp.zeros((depth, width), f32))
 
-    two = times(slab)
+    two = pack_rows(times(slab))
     slab2[me] = two.astype(bf16)
     src2 = lambda c: slab2.at[me]
     start_tasks(tasks, src2, lambda c: slab2.at[c], t2_s, t2_r)
     wait_tasks(tasks, src2, lambda c: slab2.at[c], t2_s, t2_r)
-    three = times(slab2)
+    three = pack_rows(times(slab2))
     slab3[me] = three.astype(bf16)
     src3 = lambda c: slab3.at[me]
     start_tasks(tasks, src3, lambda c: slab3.at[c], t3_s, t3_r)
+    part = -2.4375 * gram + 1.6875 * two - 0.5625 * three
     wait_tasks(tasks, src3, lambda c: slab3.at[c], t3_s, t3_r)
-    four = times(slab3)
-    poly = -2.4375 * gram + 1.6875 * two - 0.5625 * three + 0.0625 * four
-    out_ref[chip, core] = poly.astype(bf16)
-    osrc = lambda c: out_ref.at[chip, core]
-    to_chips(chips, osrc, lambda d: out_ref.at[chip, core], c_s, c_r)
-    wait_chips(chips, osrc, lambda d: out_ref.at[around(chip, chips - d, chips), core], c_s, c_r)
-    swap = remote(out_ref.at[:, core], out_ref.at[:, core], core_s.at[2], core_r.at[2], {"row": sib})
-    swap.start()
-    swap.wait_send()
-    remote(out_ref.at[:, core], out_ref.at[:, 1 - core], core_s.at[2], core_r.at[2],
-           {"row": sib}).wait_recv()
+    four = pack_rows(times(slab3))
+    final[chip, core] = (part + 0.0625 * four).astype(bf16)
+    gather(final, c_s, c_r, 2)
+    loop(0, chips * 2, lambda i: unpack_to(
+        out_ref.at[i // 2, i % 2], final[i // 2, i % 2], depth, width))
 
 
 def polynomial(partial, chips, tasks):
     total, width = partial.shape
     depth = total // (2 * chips)
     shaped = partial.reshape(chips, 2, depth, width)
+    rows = tiles(depth, width)[2]
     out = pl.pallas_call(
         functools.partial(poly_kernel, chips, tasks),
         out_shape=jax.ShapeDtypeStruct(shaped.shape, bf16),
         in_specs=[VMEM],
         out_specs=VMEM,
-        scratch_shapes=[pltpu.VMEM((chips, depth, width), bf16)] * 3
-        + [pltpu.VMEM(shaped.shape, bf16)]
-        + [pltpu.VMEM((tasks, depth, width), bf16)] * 3
+        scratch_shapes=[pltpu.VMEM((chips, depth, width), bf16)]
+        + [pltpu.VMEM((chips, rows, 128), bf16)] * 2
+        + [pltpu.VMEM((chips, 2, rows, 128), bf16), pltpu.VMEM((chips * 2, depth, width), bf16),
+           pltpu.VMEM((chips, 2, rows, 128), bf16)]
+        + [pltpu.VMEM((tasks, rows, 128), bf16)] * 3
         + [DMA((3,)), DMA((3,))] + [DMA((chips,))] * 6 + [DMA((tasks,))] * 6,
         compiler_params=params(3),
         name="polynomial",
@@ -309,59 +519,104 @@
     return out.reshape(total, width)
 
 
-def coef_kernel(chips, tasks, in_ref, w_ref, out_ref, wall_ref, sib_buf, half, slots, mine, block,
-                core_s, core_r, a_s, a_r, b_s, b_r, t1_s, t1_r, w_s, w_r):
+def pair_tiles(width):
+    return 16 * (2 * (width // 128) + (1 if width % 128 else 0))
+
+
+def pack_pair(one, two):
+    width = one.shape[1]
+    full = width // 128
+    parts = [v[:, i * 128:(i + 1) * 128] for v in (one, two) for i in range(full)]
+    if width % 128:
+        parts.append(jnp.concatenate([one[:, full * 128:], two[:, full * 128:]], axis=1))
+    return jnp.concatenate(parts, axis=0)
+
+
+def unpack_pair(packed, width):
+    full = width // 128
+    out = []
+    for v in range(2):
+        parts = [packed[(v * full + i) * 16:(v * full + i + 1) * 16] for i in range(full)]
+        if width % 128:
+            parts.append(packed[2 * full * 16:, v * 64:v * 64 + 64])
+        out.append(jnp.concatenate(parts, axis=1) if len(parts) > 1 else parts[0])
+    return out
+
+
+def coef_kernel(chips, tasks, in_ref, w_ref, out_ref, wall_ref, sib_buf, half, slots, other, other_in,
+                mine, block, gathered, wpacked, core_s, core_r, a_s, a_r, b_s, b_r, y_sem,
+                t1_s, t1_r, w_s, w_r):
     chip, core, sib = place(chips)
     me = lax.axis_index("task")
-    greet(chips, tasks, True)
+    width = in_ref.shape[-1]
+    pairs = tasks // 2
+    wdepth = w_ref.shape[0]
+    greet_near(chips, tasks)
     swap = remote(in_ref.at[:, :, 1 - core], sib_buf, core_s.at[0], core_r.at[0], {"row": sib})
     swap.start()
-    wsrc, wdst = (lambda c: w_ref), (lambda c: wall_ref.at[c])
-    start_tasks(tasks, wsrc, wdst, w_s, w_r)
+    wpacked[me] = pack_rows(w_ref[...])
+    wsteps = spread(tasks, lambda c: wpacked.at[c], w_s, w_r)
+    next(wsteps)
     wall_ref[me] = w_ref[...]
     swap.wait()
 
-    def add(u):
-        half[u] = (in_ref[u, :, core].astype(f32) + sib_buf[u].astype(f32)).astype(bf16)
-
-    loop(0, tasks, add)
-    src, dst = (lambda c: half.at[:, c]), (lambda d: slots.at[d])
-    to_chips(chips, src, dst, a_s, a_r)
-    wait_chips(chips, src, dst, a_s, a_r)
-    total = lax.fori_loop(
-        1, chips, lambda d, t: t + slots[d].astype(f32), half[:, chip].astype(f32))
-    mine[...] = total.astype(bf16)
+    def add(c):
+        for p in range(pairs):
+            one, two = (
+                in_ref[u, c, core].astype(f32) + sib_buf[u, c].astype(f32)
+                for u in (2 * p, 2 * p + 1)
+            )
+            half[c, p] = pack_pair(one, two).astype(bf16)
+
+    loop(0, chips, add)
+    total = ring_reduce(chips, half, slots, other, other_in, a_s, a_r, y_sem)
+    for p in range(pairs):
+        for v, part in enumerate(unpack_pair(total[p], width)):
+            mine[2 * p + v] = part.astype(bf16)
     block[me] = mine[me]
     tsrc, tdst = (lambda c: mine.at[c]), (lambda c: block.at[c])
     start_tasks(tasks, tsrc, tdst, t1_s, t1_r)
+    for got in wsteps:
+        unpack_to(wall_ref.at[got], wpacked[got], wdepth, width)
     wait_tasks(tasks, tsrc, tdst, t1_s, t1_r)
-    out_ref[:, chip, core] = block[...]
-    rsrc = lambda c: block
-    to_chips(chips, rsrc, lambda d: out_ref.at[:, chip, core], b_s, b_r)
-    wait_chips(chips, rsrc, lambda d: out_ref.at[:, around(chip, chips - d, chips), core], b_s, b_r)
-    swap = remote(out_ref.at[:, :, core], out_ref.at[:, :, core], core_s.at[1], core_r.at[1],
-                  {"row": sib})
+    for p in range(pairs):
+        gathered[core, chip, p] = pack_pair(block[2 * p], block[2 * p + 1])
+    ring_gather(chips, lambda c: gathered.at[core, c], b_s, b_r, y_sem)
+    swap = remote(gathered.at[core], gathered.at[core], core_s.at[1], core_r.at[1], {"row": sib})
     swap.start()
-    wait_tasks(tasks, wsrc, wdst, w_s, w_r)
+
+    def spill(which):
+        def body(c):
+            for p in range(pairs):
+                for v, part in enumerate(unpack_pair(gathered[which, c, p], width)):
+                    out_ref[2 * p + v, c, which] = part
+        loop(0, chips, body)
+
+    spill(core)
     swap.wait_send()
-    remote(out_ref.at[:, :, core], out_ref.at[:, :, 1 - core], core_s.at[1], core_r.at[1],
+    remote(gathered.at[core], gathered.at[1 - core], core_s.at[1], core_r.at[1],
            {"row": sib}).wait_recv()
+    spill(1 - core)
 
 
 def coefficients_and_weights(partial, weights, chips, tasks):
     features, width = partial.shape
     depth = features // (tasks * chips * 2)
     shaped = partial.reshape(tasks, chips, 2, depth, width)
+    chunk = (tasks // 2, pair_tiles(width), 128)
     out, wall = pl.pallas_call(
         functools.partial(coef_kernel, chips, tasks),
         out_shape=(jax.ShapeDtypeStruct(shaped.shape, bf16),
                    jax.ShapeDtypeStruct((tasks,) + weights.shape, bf16)),
         in_specs=[VMEM, VMEM],
         out_specs=(VMEM, VMEM),
-        scratch_shapes=[pltpu.VMEM((tasks, chips, depth, width), bf16)] * 2
-        + [pltpu.VMEM((chips, tasks, depth, width), bf16)]
+        scratch_shapes=[pltpu.VMEM((tasks, chips, depth, width), bf16),
+                        pltpu.VMEM((chips,) + chunk, bf16), pltpu.VMEM((chips,) + chunk, bf16),
+                        pltpu.VMEM(chunk, bf16), pltpu.VMEM(chunk, bf16)]
         + [pltpu.VMEM((tasks, depth, width), bf16)] * 2
-        + [DMA((2,)), DMA((2,))] + [DMA((chips,))] * 4 + [DMA((tasks,))] * 4,
+        + [pltpu.VMEM((2, chips) + chunk, bf16),
+           pltpu.VMEM((tasks, tiles(*weights.shape)[2], 128), bf16)]
+        + [DMA((2,)), DMA((2,))] + [DMA((chips,))] * 4 + [DMA((4,))] + [DMA((tasks,))] * 4,
         compiler_params=params(4),
         name="coefficients",
     )(shaped, weights)

time: 356 us -> 289 us (0.81)
  Pallas kernels: 326 us -> 259 us
    pallas_call x1, Pallas kernels: 111 us -> 68.9 us  [coefficients_and_weights(): pl.pallas_call(functools.partial(coef_kernel, chips, tasks), out_shape=(j...]
    pallas_call x1, Pallas kernels: 46.1 us -> 24.2 us  [gather_tasks(): pl.pallas_call(functools.partial(gather_kernel, tasks), out_shape=jax.Sha...]
where the time goes in v2:
time: 289 us
  Pallas kernels  259 us (90%)
  matrix products  17.7 us (6%)
  local copies, waits for them, and re-layouts  11 us (4%)
    pallas_call x1, Pallas kernels, polynomial(): pl.pallas_call(functools.partial(poly_kernel, chips, tasks), out_shape=ja...  104 us
    pallas_call x1, Pallas kernels, coefficients_and_weights(): pl.pallas_call(functools.partial(coef_kernel, chips, tasks), out_shape=(j...  68.9 us
    pallas_call x1, Pallas kernels, all_reduce_square(): pl.pallas_call(functools.partial(square_kernel, chips), out_shape=jax.Sha...  31.8 us
    pallas_call x1, Pallas kernels, inverse_factor(): pl.pallas_call(functools.partial(chol_kernel, blocks), out_shape=jax.Shap...  29.8 us
    pallas_call x1, Pallas kernels, gather_tasks(): pl.pallas_call(functools.partial(gather_kernel, tasks), out_shape=jax.Sha...  24.2 us

profile of v2, /device:TPU:1, one launch (start us, length us, event | category | flops | bytes accessed | tf_op | source)
XLA Modules:
  0.0 288.8 jit_solution(11903668697921332806)
XLA Ops:
  0.0 0.0 copy-start
  0.0 1.7 copy-done
  1.7 3.6 %fusion.2 = f32[448,320]{0,1:T(8,128)S(1)} fusion(bf16[1,448,4096]{2,1,0:T(8,128)(2,1)} %param.3, bf16[1,4096,320]{1,2,0:T(8,128)(2,1)S(1)} %copy-done), kind=kOutput, calls=%fused_computation.3 | convolution fusion | flops 1174405120 | bytes 6864896 | tf_op jit(solution)/shard_map/dot_general | solution.py:649
  5.3 0.0 copy-start.2
  5.3 1.2 fusion.11
  6.6 0.0 copy-done.2
  6.7 31.8 %square_sum.1 = f32[2,16,24,128]{3,2,1,0:T(8,128)S(1)} custom-call(f32[2,16,24,128]{3,2,1,0:T(8,128)S(1)} %bitcast.49), custom_call_target="tpu_custom_call" | custom-call | tf_op jit(solution)/shard_map/square_sum/pallas_call | solution.py:270
  38.5 0.1 copy.37
  38.6 0.1 copy.35
  38.7 0.1 copy.36
  38.8 0.8 select_maximum_fusion
  39.6 1.3 copy.16
  41.0 29.8 %inverse_factor.1 = f32[5,320,64]{2,1,0:T(8,128)S(1)} custom-call(f32[5,320,64]{2,1,0:T(8,128)S(1)} %bitcast.45), custom_call_target="tpu_custom_call" | custom-call | tf_op jit(solution)/shard_map/inverse_factor/pallas_call | solution.py:329
  70.8 0.0 copy-start.1
  70.8 0.9 copy-done.1
  71.7 1.5 copy.17
  73.1 2.7 multiply_convert_fusion
  75.8 24.2 %basis_gather.1 = bf16[8,448,320]{2,1,0:T(8,128)(2,1)S(1)} custom-call(bf16[448,320]{1,0:T(8,128)(2,1)S(1)} %get-tuple-element.9.in_ref), custom_call_target="tpu_custom_call" | custom-call | tf_op jit(solution)/shard_map/basis_gather/pallas_call | solution.py:422
  100.0 1.6 convolution_convert_fusion.1
  101.6 104.4 %polynomial.1 = bf16[16,2,80,320]{3,2,1,0:T(8,128)(2,1)S(1)} custom-call(bf16[16,2,80,320]{3,2,1,0:T(8,128)(2,1)S(1)} %bitcast.48), custom_call_target="tpu_custom_call" | custom-call | tf_op jit(solution)/shard_map/polynomial/pallas_call | solution.py:505
  205.9 0.0 copy-start.3
  205.9 1.4 fusion.8.w_ref
  207.3 0.7 copy-done.3
  208.0 3.1 %fusion = bf16[4096,320]{0,1:T(8,128)(2,1)} fusion(bf16[448,320]{1,0:T(8,128)(2,1)S(1)} %fusion.8.w_ref, bf16[1,448,4096]{2,1,0:T(8,128)(2,1)S(1)} %copy-done.3), kind=kOutput, calls=%fused_computation.1 | convolution fusion | flops 1175715840 | bytes 6578176 | tf_op jit(solution)/shard_map/dot_general | solution.py:667
  211.1 4.6 %copy.24 = bf16[4096,320]{1,0:T(8,128)(2,1)} copy(bf16[4096,320]{0,1:T(8,128)(2,1)} %fusion) | data formatting | bytes 5242880 | tf_op jit(solution)/shard_map/convert_element_type | solution.py:669
  215.6 0.0 copy-start.4
  215.6 68.9 %coefficients.1 = (bf16[8,16,2,16,320]{4,3,2,1,0:T(8,128)(2,1)}, bf16[8,448,320]{2,1,0:T(8,128)(2,1)S(1)}) custom-call(bf16[8,16,2,16,320]{4,3,2,1,0:T(8,128)(2,1)} %bitcast.53, bf16[448,320]{1,0:T(8,128)(2,1)S(1)} %fusion.8.w_ref), custom_call_target="tpu_custom_call" | custom-call | tf_op jit(solution)/shard_map/coefficients/pallas_call | solution.py:607
  284.5 0.0 copy-done.4
  284.5 4.3 %fusion.6 = bf16[448,512]{1,0:T(8,128)(2,1)} fusion(bf16[8,448,320]{2,1,0:T(8,128)(2,1)S(1)} %get-tuple-element.7, bf16[8,512,320]{2,1,0:T(8,128)(2,1)} %bitcast.56, bf16[448,512]{1,0:T(8,128)(2,1)S(1)} %copy-done.4), kind=kOutput, calls=%fused_computation.9 | convolution fusion | flops 1175093248 | bytes 5832704 | tf_op jit(solution)/shard_map/dot_general | solution.py:671
  (8 shorter events, 0.1 us)
Async XLA Ops:
  0.0 1.7 copy-start
  5.3 1.3 copy-start.2
  70.8 0.9 copy-start.1
  205.9 2.0 copy-start.3
  215.6 68.9 %copy-start.4 = (bf16[448,512]{1,0:T(8,128)(2,1)S(1)}, bf16[448,512]{1,0:T(8,128)(2,1)}, u32[]{:S(2)}) copy-start(bf16[448,512]{1,0:T(8,128)(2,1)} %param.5) | copy-start | bytes 1376260

commit v3 on v2

--- a/solution.py
+++ b/solution.py
@@ -15,6 +15,7 @@
 f32 = jnp.float32
 bf16 = jnp.bfloat16
 CB = 64
+PANEL = 8
 
 
 def params(cid):
@@ -125,16 +126,19 @@
         dst[top:, full * 128:] = tail[:depth - top, 64:]
 
 
-def greet_near(chips, tasks):
+def hello(chips, tasks):
     barrier = pltpu.get_barrier_semaphore()
     chip, core, sib = place(chips)
-    zs, z, y = chips // 2, chip // 2, chip % 2
-    for there in (sib, line(zs, z + 1, y, core), line(zs, z - 1, y, core), line(zs, z, 1 - y, core)):
-        pl.semaphore_signal(barrier, inc=1, device_id={"row": there}, device_id_type=MESH)
+    pl.semaphore_signal(barrier, inc=1, device_id={"row": sib}, device_id_type=MESH)
+    loop(1, chips, lambda d: pl.semaphore_signal(
+        barrier, inc=1, device_id={"row": around(chip, d, chips) * 2 + core}, device_id_type=MESH))
     me = lax.axis_index("task")
     loop(1, tasks, lambda d: pl.semaphore_signal(
         barrier, inc=1, device_id={"task": around(me, d, tasks)}, device_id_type=MESH))
-    pl.semaphore_wait(barrier, 4 + tasks - 1)
+
+
+def barrier_wait(chips, tasks):
+    pl.semaphore_wait(pltpu.get_barrier_semaphore(), chips + tasks - 1)
 
 
 def line(zs, z, y, core):
@@ -290,22 +294,31 @@
                            preferred_element_type=f32)
 
 
-def chol_kernel(blocks, a_ref, z_ref, cols, fac, inv):
+def basis_kernel(shrink, packed, x_ref, own_ref, cols, fac, inv):
+    n = x_ref.shape[1]
+    blocks = n // CB
     row_id = lax.broadcasted_iota(jnp.int32, (CB, 2 * CB), 0)
     lane_id = lax.broadcasted_iota(jnp.int32, (CB, 2 * CB), 1)
     eye = (lane_id == row_id + CB).astype(f32)
     inv[...] = jnp.zeros_like(inv)
-    cols[...] = a_ref[...]
+    for k in range(blocks):
+        wide, off = divmod(k * CB, 128)
+        top = sum(n - 128 * w for w in range(wide))
+        cols[k, k * CB:, :] = packed[top + off:top + n - 128 * wide, off:off + CB]
     for k in range(blocks):
         at = k * CB
         both = jnp.concatenate([cols[k, at:at + CB, :], jnp.zeros((CB, CB), f32)], axis=1) + eye
-        for j in range(CB):
-            scale = lax.rsqrt(both[j:j + 1, j:j + 1])
-            line = both[j:j + 1, :] * scale
-            down = both[:, j:j + 1] * scale
-            below = both - down * line
-            both = jnp.where(row_id > j, below, jnp.where(row_id == j, line, both))
-        zkk = both[:, CB:]
+        for first in range(0, CB, PANEL):
+            wide = [jnp.broadcast_to(both[:, first + m:first + m + 1], both.shape)
+                    for m in range(PANEL)]
+            for m in range(PANEL):
+                j = first + m
+                f = jnp.where(row_id > j, wide[m] * (1.0 / wide[m][j:j + 1, :]), 0.0)
+                for q in range(m + 1, PANEL):
+                    wide[q] = wide[q] - f * wide[q][j:j + 1, :]
+                both = both - f * both[j:j + 1, :]
+        diag = jnp.sum(jnp.where(lane_id == row_id, both, 0.0), axis=1, keepdims=True)
+        zkk = both[:, CB:] * lax.rsqrt(diag)
         if k + 1 < blocks:
             panel = dot_nt(cols[k, at + CB:, :], zkk)
             fac[k, at + CB:, :] = panel
@@ -319,23 +332,21 @@
                 acc = acc + dot_nn(fac[m, at:at + CB, :], inv[c, m * CB:(m + 1) * CB, :])
             inv[c, at:at + CB, :] = -dot_nn(zkk, acc)
         inv[k, at:at + CB, :] = zkk
-    z_ref[...] = inv[...]
-
-
-def inverse_factor(square):
-    n = square.shape[0]
-    blocks = n // CB
-    a = jnp.transpose(square.reshape(n, blocks, CB), (1, 0, 2))
-    z = pl.pallas_call(
-        functools.partial(chol_kernel, blocks),
-        out_shape=jax.ShapeDtypeStruct((blocks, n, CB), f32),
-        in_specs=[VMEM],
+    z = jnp.concatenate([inv[c] for c in range(blocks)], axis=1)
+    own_ref[...] = dot_nt(x_ref[...], z) * shrink
+
+
+def basis_of(packed, sketched, shrink):
+    n = sketched.shape[1]
+    return pl.pallas_call(
+        functools.partial(basis_kernel, shrink),
+        out_shape=jax.ShapeDtypeStruct(sketched.shape, f32),
+        in_specs=[VMEM, VMEM],
         out_specs=VMEM,
-        scratch_shapes=[pltpu.VMEM((blocks, n, CB), f32)] * 3,
+        scratch_shapes=[pltpu.VMEM((n // CB, n, CB), f32)] * 3,
         compiler_params=pltpu.CompilerParams(vmem_limit_bytes=32 * 1024 * 1024),
-        name="inverse_factor",
-    )(a)
-    return jnp.transpose(z, (1, 0, 2)).reshape(n, n)
+        name="basis",
+    )(packed, sketched)
 
 
 def start_tasks(tasks, src, dst, ssem, rsem):
@@ -405,78 +416,122 @@
         copy.wait_send()
 
 
-def gather_kernel(tasks, in_ref, out_ref, packed, a_s, a_r):
-    me = lax.axis_index("task")
-    depth, width = in_ref.shape
-    greet(0, tasks, False)
-    packed[me] = pack_rows(in_ref[...])
-    steps = spread(tasks, lambda c: packed.at[c], a_s, a_r)
-    next(steps)
-    out_ref[me] = in_ref[...]
-    for got in steps:
-        unpack_to(out_ref.at[got], packed[got], depth, width)
-
-
-def gather_tasks(block, tasks):
-    rows = tiles(*block.shape)[2]
-    return pl.pallas_call(
-        functools.partial(gather_kernel, tasks),
-        out_shape=jax.ShapeDtypeStruct((tasks,) + block.shape, block.dtype),
-        in_specs=[VMEM],
-        out_specs=VMEM,
-        scratch_shapes=[pltpu.VMEM((tasks, rows, 128), block.dtype), DMA((tasks,)), DMA((tasks,))],
-        compiler_params=params(2),
-        name="basis_gather",
-    )(block)
-
-
-def poly_kernel(chips, tasks, in_ref, out_ref, sib_buf, half, slots, column, matrix, final, slab, slab2, slab3,
-                core_s, core_r, a_s, a_r, b_s, b_r, c_s, c_r, t1_s, t1_r, t2_s, t2_r, t3_s, t3_r):
+def pair_tiles(width):
+    return 16 * (2 * (width // 128) + (1 if width % 128 else 0))
+
+
+def pack_pair(one, two):
+    width = one.shape[1]
+    full = width // 128
+    parts = [v[:, i * 128:(i + 1) * 128] for v in (one, two) for i in range(full)]
+    if width % 128:
+        parts.append(jnp.concatenate([one[:, full * 128:], two[:, full * 128:]], axis=1))
+    return jnp.concatenate(parts, axis=0)
+
+
+def unpack_pair(packed, width):
+    full = width // 128
+    out = []
+    for v in range(2):
+        parts = [packed[(v * full + i) * 16:(v * full + i + 1) * 16] for i in range(full)]
+        if width % 128:
+            parts.append(packed[2 * full * 16:, v * 64:v * 64 + 64])
+        out.append(jnp.concatenate(parts, axis=1) if len(parts) > 1 else parts[0])
+    return out
+
+
+def joint_kernel(
+    chips, tasks, own_ref, delta_hbm, out_ref, wall_ref,
+    delta, turned, stack, packed, terms, sib_buf, half, slots, column, matrix, final,
+    slab, slab2, slab3, parts, sib_parts, half2, slots2, other, other_in, mine, block, gathered, wpacked,
+    local_s, g_s, g_r, sw_s, sw_r, core_s, core_r, a_s, a_r, b_s, b_r, c_s, c_r,
+    t1_s, t1_r, t2_s, t2_r, t3_s, t3_r, w_s, w_r, sp_s, sp_r, d_s, d_r, e_s, e_r, y_sem, t4_s, t4_r,
+):
     chip, core, sib = place(chips)
     me = lax.axis_index("task")
-    depth, width = in_ref.shape[2:]
+    rows, width = own_ref.shape
+    depth = terms.shape[2]
     per = width // depth
-    greet(chips, tasks, True)
-    swap = remote(in_ref.at[:, 1 - core], sib_buf, core_s.at[0], core_r.at[0], {"row": sib})
-    swap.start()
-    swap.wait()
-
-    def add(c):
-        both = in_ref[c, core].astype(f32) + sib_buf[c].astype(f32)
-        half[c] = pack_rows(both).astype(bf16)
-
-    loop(0, chips, add)
-    src, dst = (lambda c: half.at[c]), (lambda d: slots.at[d])
-    to_chips(chips, src, dst, a_s, a_r)
-    wait_chips(chips, src, dst, a_s, a_r)
+    pairs = tasks // 2
+    hello(chips, tasks)
+    load = pltpu.make_async_copy(delta_hbm, delta, local_s.at[0])
+    load.start()
+    own = own_ref[...].astype(bf16)
+    stack[me] = own
+    packed[me] = pack_rows(own)
+    barrier_wait(chips, tasks)
+
+    def swap_term(s, i):
+        at = pl.ds(s * (per // 2), per // 2)
+        return remote(terms.at[at, 1 - core], sib_buf.at[at], sw_s.at[i], sw_r.at[i], {"row": sib})
+
+    def gram_term(s, i):
+        term = lax.dot_general(stack[s], stack[me], (((0,), (0,)), ((), ())),
+                               preferred_element_type=f32).astype(bf16)
+        terms[pl.ds(s * (per // 2), per // 2)] = term.reshape(per // 2, 2, depth, width)
+        swap_term(s, i).start()
+
+    def to_owner(s, i):
+        swap_term(s, i).wait()
+        for e in range(per // 2):
+            c = s * (per // 2) + e
+            both = terms[c, core].astype(f32) + sib_buf[c].astype(f32)
+            half[c] = pack_rows(both).astype(bf16)
+            d = around(c, chips - chip, chips)
+
+            @pl.when(c != chip)
+            def _():
+                remote(half.at[c], slots.at[d], a_s.at[d], a_r.at[d], {"row": c * 2 + core}).start()
+
+    steps = spread(tasks, lambda c: packed.at[c], g_s, g_r)
+    next(steps)
+    gram_term(me, 0)
+    ready = [me]
+    for got in steps:
+        unpack_to(stack.at[got], packed[got], rows, width)
+        ready.append(got)
+        gram_term(got, len(ready) - 1)
+        to_owner(ready[-2], len(ready) - 2)
+    to_owner(ready[-1], len(ready) - 1)
+    wait_chips(chips, lambda c: half.at[c], lambda d: slots.at[d], a_s, a_r)
     gram = lax.fori_loop(
         1, chips, lambda d, t: t + slots[d].astype(f32), half[chip].astype(f32))
-    mine = gram.astype(bf16)
-    slab[me] = mine
-    column[chip, core] = mine
+    first = gram.astype(bf16)
+    slab[me] = first
+    column[chip, core] = first
+
     tsrc = lambda c: slab.at[me]
     start_tasks(tasks, tsrc, lambda c: slab.at[c], t1_s, t1_r)
 
-    def gather(buf, sems, recvs, n):
-        block = lambda c: buf.at[chip, core]
-        to_chips(chips, block, lambda d: buf.at[chip, core], sems, recvs)
-        wait_chips(chips, block, lambda d: buf.at[around(chip, chips - d, chips), core], sems, recvs)
+    def gather(buf, sems, recvs, n, beside):
+        mine_at = lambda c: buf.at[chip, core]
+        to_chips(chips, mine_at, lambda d: buf.at[chip, core], sems, recvs)
+        beside()
+        wait_chips(chips, mine_at, lambda d: buf.at[around(chip, chips - d, chips), core], sems, recvs)
         swap = remote(buf.at[:, core], buf.at[:, core], core_s.at[n], core_r.at[n], {"row": sib})
         swap.start()
         swap.wait_send()
         remote(buf.at[:, core], buf.at[:, 1 - core], core_s.at[n], core_r.at[n],
                {"row": sib}).wait_recv()
 
-    gather(column, b_s, b_r, 1)
+    span = turned.shape[0] // tasks
+
+    def turn():
+        load.wait()
+        loop(0, tasks, lambda u: turned.__setitem__(
+            pl.ds(pl.multiple_of(u * span, span), span),
+            delta[:, pl.ds(pl.multiple_of(u * span, span), span)].T))
+
+    gather(column, b_s, b_r, 1, turn)
     loop(0, chips * 2, lambda i: unpack_to(
         matrix.at[i], column[i // 2, i % 2], depth, width))
     wait_tasks(tasks, tsrc, lambda c: slab.at[c], t1_s, t1_r)
 
     def times(left):
         def body(s, total):
-            block = matrix[pl.ds(s * per, per)].reshape(width, width)
+            right = matrix[pl.ds(s * per, per)].reshape(width, width)
             return total + jnp.dot(
-                unpack_rows(left[s], depth, width), block, preferred_element_type=f32)
+                unpack_rows(left[s], depth, width), right, preferred_element_type=f32)
         return lax.fori_loop(0, tasks, body, jnp.zeros((depth, width), f32))
 
     two = pack_rows(times(slab))
@@ -490,137 +545,103 @@
     start_tasks(tasks, src3, lambda c: slab3.at[c], t3_s, t3_r)
     part = -2.4375 * gram + 1.6875 * two - 0.5625 * three
     wait_tasks(tasks, src3, lambda c: slab3.at[c], t3_s, t3_r)
-    four = pack_rows(times(slab3))
-    final[chip, core] = (part + 0.0625 * four).astype(bf16)
-    gather(final, c_s, c_r, 2)
+    final[chip, core] = (part + 0.0625 * pack_rows(times(slab3))).astype(bf16)
+    gather(final, c_s, c_r, 2, lambda: None)
     loop(0, chips * 2, lambda i: unpack_to(
-        out_ref.at[i // 2, i % 2], final[i // 2, i % 2], depth, width))
-
-
-def polynomial(partial, chips, tasks):
-    total, width = partial.shape
-    depth = total // (2 * chips)
-    shaped = partial.reshape(chips, 2, depth, width)
-    rows = tiles(depth, width)[2]
-    out = pl.pallas_call(
-        functools.partial(poly_kernel, chips, tasks),
-        out_shape=jax.ShapeDtypeStruct(shaped.shape, bf16),
-        in_specs=[VMEM],
-        out_specs=VMEM,
-        scratch_shapes=[pltpu.VMEM((chips, depth, width), bf16)]
-        + [pltpu.VMEM((chips, rows, 128), bf16)] * 2
-        + [pltpu.VMEM((chips, 2, rows, 128), bf16), pltpu.VMEM((chips * 2, depth, width), bf16),
-           pltpu.VMEM((chips, 2, rows, 128), bf16)]
-        + [pltpu.VMEM((tasks, rows, 128), bf16)] * 3
-        + [DMA((3,)), DMA((3,))] + [DMA((chips,))] * 6 + [DMA((tasks,))] * 6,
-        compiler_params=params(3),
-        name="polynomial",
-    )(shaped)
-    return out.reshape(total, width)
-
-
-def pair_tiles(width):
-    return 16 * (2 * (width // 128) + (1 if width % 128 else 0))
-
-
-def pack_pair(one, two):
-    width = one.shape[1]
-    full = width // 128
-    parts = [v[:, i * 128:(i + 1) * 128] for v in (one, two) for i in range(full)]
-    if width % 128:
-        parts.append(jnp.concatenate([one[:, full * 128:], two[:, full * 128:]], axis=1))
-    return jnp.concatenate(parts, axis=0)
-
-
-def unpack_pair(packed, width):
-    full = width // 128
-    out = []
-    for v in range(2):
-        parts = [packed[(v * full + i) * 16:(v * full + i + 1) * 16] for i in range(full)]
-        if width % 128:
-            parts.append(packed[2 * full * 16:, v * 64:v * 64 + 64])
-        out.append(jnp.concatenate(parts, axis=1) if len(parts) > 1 else parts[0])
-    return out
-
-
-def coef_kernel(chips, tasks, in_ref, w_ref, out_ref, wall_ref, sib_buf, half, slots, other, other_in,
-                mine, block, gathered, wpacked, core_s, core_r, a_s, a_r, b_s, b_r, y_sem,
-                t1_s, t1_r, w_s, w_r):
-    chip, core, sib = place(chips)
-    me = lax.axis_index("task")
-    width = in_ref.shape[-1]
-    pairs = tasks // 2
-    wdepth = w_ref.shape[0]
-    greet_near(chips, tasks)
-    swap = remote(in_ref.at[:, :, 1 - core], sib_buf, core_s.at[0], core_r.at[0], {"row": sib})
-    swap.start()
-    wpacked[me] = pack_rows(w_ref[...])
+        matrix.at[i], final[i // 2, i % 2], depth, width))
+
+    def apply(s, total):
+        right = matrix[pl.ds(s * per, per)].reshape(width, width)
+        return total + jnp.dot(stack[s], right, preferred_element_type=f32)
+
+    weights = lax.fori_loop(0, tasks, apply, 2.25 * own_ref[...]).astype(bf16)
+    wall_ref[me] = weights
+    wpacked[me] = pack_rows(weights)
     wsteps = spread(tasks, lambda c: wpacked.at[c], w_s, w_r)
     next(wsteps)
-    wall_ref[me] = w_ref[...]
-    swap.wait()
+
+    def swap_part(u):
+        return remote(parts.at[u, :, 1 - core], sib_parts.at[u], sp_s.at[u], sp_r.at[u], {"row": sib})
+
+    def coef_term(u):
+        rows_u = turned[pl.ds(pl.multiple_of(u * span, span), span)]
+        term = jnp.dot(rows_u, wall_ref[me], preferred_element_type=f32).astype(bf16)
+        parts[u] = term.reshape(parts.shape[1:])
+        swap_part(u).start()
+
+    loop(0, tasks, coef_term)
+    loop(0, tasks, lambda u: swap_part(u).wait())
 
     def add(c):
         for p in range(pairs):
             one, two = (
-                in_ref[u, c, core].astype(f32) + sib_buf[u, c].astype(f32)
+                parts[u, c, core].astype(f32) + sib_parts[u, c].astype(f32)
                 for u in (2 * p, 2 * p + 1)
             )
-            half[c, p] = pack_pair(one, two).astype(bf16)
+            half2[c, p] = pack_pair(one, two).astype(bf16)
 
     loop(0, chips, add)
-    total = ring_reduce(chips, half, slots, other, other_in, a_s, a_r, y_sem)
+    total = ring_reduce(chips, half2, slots2, other, other_in, d_s, d_r, y_sem)
     for p in range(pairs):
-        for v, part in enumerate(unpack_pair(total[p], width)):
-            mine[2 * p + v] = part.astype(bf16)
+        for v, piece in enumerate(unpack_pair(total[p], width)):
+            mine[2 * p + v] = piece.astype(bf16)
     block[me] = mine[me]
-    tsrc, tdst = (lambda c: mine.at[c]), (lambda c: block.at[c])
-    start_tasks(tasks, tsrc, tdst, t1_s, t1_r)
+    tsrc4, tdst4 = (lambda c: mine.at[c]), (lambda c: block.at[c])
+    start_tasks(tasks, tsrc4, tdst4, t4_s, t4_r)
     for got in wsteps:
-        unpack_to(wall_ref.at[got], wpacked[got], wdepth, width)
-    wait_tasks(tasks, tsrc, tdst, t1_s, t1_r)
+        unpack_to(wall_ref.at[got], wpacked[got], rows, width)
+    wait_tasks(tasks, tsrc4, tdst4, t4_s, t4_r)
     for p in range(pairs):
         gathered[core, chip, p] = pack_pair(block[2 * p], block[2 * p + 1])
-    ring_gather(chips, lambda c: gathered.at[core, c], b_s, b_r, y_sem)
-    swap = remote(gathered.at[core], gathered.at[core], core_s.at[1], core_r.at[1], {"row": sib})
+    ring_gather(chips, lambda c: gathered.at[core, c], e_s, e_r, y_sem)
+    swap = remote(gathered.at[core], gathered.at[core], core_s.at[0], core_r.at[0], {"row": sib})
     swap.start()
 
     def spill(which):
         def body(c):
             for p in range(pairs):
-                for v, part in enumerate(unpack_pair(gathered[which, c, p], width)):
-                    out_ref[2 * p + v, c, which] = part
+                for v, piece in enumerate(unpack_pair(gathered[which, c, p], width)):
+                    out_ref[2 * p + v, c, which] = piece
         loop(0, chips, body)
 
     spill(core)
     swap.wait_send()
-    remote(gathered.at[core], gathered.at[1 - core], core_s.at[1], core_r.at[1],
+    remote(gathered.at[core], gathered.at[1 - core], core_s.at[0], core_r.at[0],
            {"row": sib}).wait_recv()
     spill(1 - core)
 
 
-def coefficients_and_weights(partial, weights, chips, tasks):
-    features, width = partial.shape
-    depth = features // (tasks * chips * 2)
-    shaped = partial.reshape(tasks, chips, 2, depth, width)
+def joint(own, delta, chips, tasks):
+    rows, width = own.shape
+    features = delta.shape[1]
+    depth = tasks * width // (2 * chips)
+    piece = features // (tasks * chips * 2)
     chunk = (tasks // 2, pair_tiles(width), 128)
-    out, wall = pl.pallas_call(
-        functools.partial(coef_kernel, chips, tasks),
-        out_shape=(jax.ShapeDtypeStruct(shaped.shape, bf16),
-                   jax.ShapeDtypeStruct((tasks,) + weights.shape, bf16)),
-        in_specs=[VMEM, VMEM],
+    high = tiles(depth, width)[2]
+    tall = tiles(rows, width)[2]
+    buf = lambda *shape: pltpu.VMEM(shape, bf16)
+    pair = lambda n: [DMA((n,)), DMA((n,))]
+    return pl.pallas_call(
+        functools.partial(joint_kernel, chips, tasks),
+        out_shape=(jax.ShapeDtypeStruct((tasks, chips, 2, piece, width), bf16),
+                   jax.ShapeDtypeStruct((tasks, rows, width), bf16)),
+        in_specs=[VMEM, pl.BlockSpec(memory_space=pl.ANY)],
         out_specs=(VMEM, VMEM),
-        scratch_shapes=[pltpu.VMEM((tasks, chips, depth, width), bf16),
-                        pltpu.VMEM((chips,) + chunk, bf16), pltpu.VMEM((chips,) + chunk, bf16),
-                        pltpu.VMEM(chunk, bf16), pltpu.VMEM(chunk, bf16)]
-        + [pltpu.VMEM((tasks, depth, width), bf16)] * 2
-        + [pltpu.VMEM((2, chips) + chunk, bf16),
-           pltpu.VMEM((tasks, tiles(*weights.shape)[2], 128), bf16)]
-        + [DMA((2,)), DMA((2,))] + [DMA((chips,))] * 4 + [DMA((4,))] + [DMA((tasks,))] * 4,
-        compiler_params=params(4),
-        name="coefficients",
-    )(shaped, weights)
-    return out.reshape(tasks, features // tasks, width), wall
+        scratch_shapes=[
+            buf(rows, features), buf(features, rows), buf(tasks, rows, width), buf(tasks, tall, 128),
+            buf(chips, 2, depth, width), buf(chips, depth, width), buf(chips, high, 128),
+            buf(chips, high, 128), buf(chips, 2, high, 128), buf(chips * 2, depth, width),
+            buf(chips, 2, high, 128),
+            buf(tasks, high, 128), buf(tasks, high, 128), buf(tasks, high, 128),
+            buf(tasks, chips, 2, piece, width), buf(tasks, chips, piece, width),
+            buf(chips, *chunk), buf(chips, *chunk), buf(*chunk), buf(*chunk),
+            buf(tasks, piece, width), buf(tasks, piece, width), buf(2, chips, *chunk),
+            buf(tasks, tall, 128), DMA((1,)),
+        ] + pair(tasks) + pair(tasks) + pair(3) + pair(chips) * 3
+        + pair(tasks) * 5 + pair(chips) * 2 + [DMA((4,))] + pair(tasks),
+        compiler_params=params(2),
+        name="joint",
+    )(own, delta)
 
 
 def pack(square):
@@ -630,15 +651,6 @@
         piece = square[at:, at:min(at + 128, n)]
         parts.append(jnp.pad(piece, ((0, 0), (0, 128 - piece.shape[1]))))
     return jnp.concatenate(parts, axis=0)
-
-
-def unpack(packed, n):
-    parts, top = [], 0
-    for at in range(0, n, 128):
-        piece = packed[top:top + n - at, :min(128, n - at)]
-        parts.append(jnp.pad(piece, ((at, 0), (0, 0))))
-        top += n - at
-    return jnp.concatenate(parts, axis=1)
 
 
 def local(delta, sketch, base):
@@ -650,26 +662,12 @@
     packed = pack(jnp.dot(sketched.T, sketched, precision=highest))
     unit = 16 * chips
     packed = jnp.pad(packed, ((0, -packed.shape[0] % unit), (0, 0)))
-    square = unpack(all_reduce_square(packed, chips), width)
-    inverse = inverse_factor(square)
-    own = lax.dot_general(
-        sketched, inverse, (((1,), (1,)), ((), ())), precision=highest
-    ) * (1.0 / math.sqrt(tasks))
-    stack = gather_tasks(own.astype(bf16), tasks)
-    gram = lax.dot_general(
-        stack, own.astype(bf16), (((1,), (0,)), ((), ())), preferred_element_type=f32
-    ).reshape(tasks * width, width).astype(bf16)
-    poly = polynomial(gram, chips, tasks).reshape(tasks, width, width)
-    weights = (
-        2.25 * own
-        + lax.dot_general(stack, poly, (((0, 2), (0, 1)), ((), ())), preferred_element_type=f32)
-    ).astype(bf16)
-    partial = lax.dot_general(
-        delta_rows, weights, (((0,), (0,)), ((), ())), preferred_element_type=f32
-    ).astype(bf16)
-    coefs, stack2 = coefficients_and_weights(partial, weights, chips, tasks)
+    packed = all_reduce_square(packed, chips)
+    own = basis_of(packed, sketched, 1.0 / math.sqrt(tasks))
+    coefs, stack = joint(own, delta_rows, chips, tasks)
+    coefs = coefs.reshape(tasks, -1, width)
     update = lax.dot_general(
-        stack2, coefs, (((0, 2), (0, 2)), ((), ())), preferred_element_type=f32
+        stack, coefs, (((0, 2), (0, 2)), ((), ())), preferred_element_type=f32
     )
     return (base.astype(f32) + update).astype(bf16)
 

time: 289 us -> 261 us (0.903)
  Pallas kernels: 259 us -> 244 us
  matrix products: 17.7 us -> 9.82 us
  local copies, waits for them, and re-layouts: 11 us -> 6.52 us
    pallas_call x4 -> x2, Pallas kernels: 227 us -> 213 us  [the longest x1 199 us: joint(): pl.pallas_call(functools.partial(joint_kernel, chips, tasks), out_shape=(...]
    dot_general x5 -> x1, matrix products: 13 us -> 4.28 us  [local(): lax.dot_general(stack, coefs, (((0, 2), (0, 2)), ((), ())), preferred_ele...]
    convert_element_type x1 -> x0, local copies, waits for them, and re-layouts: 4.55 us -> none  [local(): partial = lax.dot_general(delta_rows, weights, (((0,), (0,)), ((), ())),...]
where the time goes in v3:
time: 261 us
  Pallas kernels  244 us (93%)
  matrix products  9.82 us (4%)
  local copies, waits for them, and re-layouts  6.52 us (2%)
    pallas_call x1, Pallas kernels, joint(): pl.pallas_call(functools.partial(joint_kernel, chips, tasks), out_shape=(...  199 us
    pallas_call x1, Pallas kernels, all_reduce_square(): pl.pallas_call(functools.partial(square_kernel, chips), out_shape=jax.Sha...  31.8 us
    pallas_call x1, Pallas kernels, basis_of(): pl.pallas_call(functools.partial(basis_kernel, shrink), out_shape=jax.Sha...  13.5 us

profile of v3, /device:TPU:1, one launch (start us, length us, event | category | flops | bytes accessed | tf_op | source)
XLA Modules:
  0.0 260.9 jit_solution(15312221109945901951)
XLA Ops:
  0.0 0.0 copy-start
  0.0 1.7 copy-done
  1.7 3.6 %fusion = f32[448,320]{0,1:T(8,128)S(1)} fusion(bf16[1,4096,320]{1,2,0:T(8,128)(2,1)S(1)} %copy-done, bf16[1,448,4096]{2,1,0:T(8,128)(2,1)} %param.3), kind=kOutput, calls=%fused_computation | convolution fusion | flops 1174405120 | bytes 6864896 | tf_op jit(solution)/shard_map/dot_general | solution.py:661
  5.3 0.0 copy-start.1
  5.3 0.8 copy-done.1
  6.2 2.0 fusion.5
  8.1 1.3 copy.4.x_ref
  9.5 0.8 slice.14
  10.2 0.9 slice.13
  11.1 0.9 slice.12
  12.1 31.8 %square_sum.1 = f32[2,16,24,128]{3,2,1,0:T(8,128)S(1)} custom-call(f32[2,16,24,128]{3,2,1,0:T(8,128)S(1)} %bitcast.19), custom_call_target="tpu_custom_call" | custom-call | tf_op jit(solution)/shard_map/square_sum/pallas_call | solution.py:274
  43.9 0.0 copy-start.2
  43.9 13.5 %basis.1.own_ref = f32[448,320]{1,0:T(8,128)S(1)} custom-call(f32[768,128]{1,0:T(8,128)S(1)} %bitcast.20, f32[448,320]{1,0:T(8,128)S(1)} %copy.4.x_ref), custom_call_target="tpu_custom_call" | custom-call | tf_op jit(solution)/shard_map/basis/pallas_call | solution.py:341
  57.4 199.2 %joint.1 = (bf16[8,16,2,16,320]{4,3,2,1,0:T(8,128)(2,1)}, bf16[8,448,320]{2,1,0:T(8,128)(2,1)S(1)}) custom-call(f32[448,320]{1,0:T(8,128)S(1)} %basis.1.own_ref, bf16[448,4096]{1,0:T(8,128)(2,1)} %bitcast.21), custom_call_target="tpu_custom_call" | custom-call | tf_op jit(solution)/shard_map/joint/pallas_call | solution.py:624
  256.6 0.0 copy-done.2
  256.6 4.3 %fusion.3 = bf16[448,512]{1,0:T(8,128)(2,1)} fusion(bf16[8,448,320]{2,1,0:T(8,128)(2,1)S(1)} %get-tuple-element.7, bf16[8,512,320]{2,1,0:T(8,128)(2,1)} %bitcast.22, bf16[448,512]{1,0:T(8,128)(2,1)S(1)} %copy-done.2), kind=kOutput, calls=%fused_computation.4 | convolution fusion | flops 1175093248 | bytes 5832704 | tf_op jit(solution)/shard_map/dot_general | solution.py:669
  (2 shorter events, 0.1 us)
Async XLA Ops:
  0.0 1.7 copy-start
  5.3 0.8 copy-start.1
  43.9 212.7 %copy-start.2 = (bf16[448,512]{1,0:T(8,128)(2,1)S(1)}, bf16[448,512]{1,0:T(8,128)(2,1)}, u32[]{:S(2)}) copy-start(bf16[448,512]{1,0:T(8,128)(2,1)} %param.5) | copy-start | bytes 1376260

commit v4 on v3

--- a/solution.py
+++ b/solution.py
@@ -16,6 +16,7 @@
 bf16 = jnp.bfloat16
 CB = 64
 PANEL = 8
+LOADS = 4
 
 
 def params(cid):
@@ -47,24 +48,6 @@
         return carry
 
     lax.fori_loop(lo, hi, step, 0)
-
-
-def greet(chips, tasks, rows):
-    barrier = pltpu.get_barrier_semaphore()
-    total = 0
-    if rows:
-        chip, core, sib = place(chips)
-        pl.semaphore_signal(barrier, inc=1, device_id={"row": sib}, device_id_type=MESH)
-        loop(1, chips, lambda d: pl.semaphore_signal(
-            barrier, inc=1, device_id={"row": around(chip, d, chips) * 2 + core},
-            device_id_type=MESH))
-        total += chips
-    if tasks:
-        me = lax.axis_index("task")
-        loop(1, tasks, lambda d: pl.semaphore_signal(
-            barrier, inc=1, device_id={"task": around(me, d, tasks)}, device_id_type=MESH))
-        total += tasks - 1
-    pl.semaphore_wait(barrier, total)
 
 
 def to_chips(chips, src, dst, ssem, rsem):
@@ -132,9 +115,10 @@
     pl.semaphore_signal(barrier, inc=1, device_id={"row": sib}, device_id_type=MESH)
     loop(1, chips, lambda d: pl.semaphore_signal(
         barrier, inc=1, device_id={"row": around(chip, d, chips) * 2 + core}, device_id_type=MESH))
-    me = lax.axis_index("task")
-    loop(1, tasks, lambda d: pl.semaphore_signal(
-        barrier, inc=1, device_id={"task": around(me, d, tasks)}, device_id_type=MESH))
+    if tasks:
+        me = lax.axis_index("task")
+        loop(1, tasks, lambda d: pl.semaphore_signal(
+            barrier, inc=1, device_id={"task": around(me, d, tasks)}, device_id_type=MESH))
 
 
 def barrier_wait(chips, tasks):
@@ -201,7 +185,7 @@
     return own + other_in[...].astype(f32)
 
 
-def ring_gather(chips, at, ssem, rsem, ysem):
+def ring_gather(chips, at, ssem, rsem, ysem, landed):
     chip, core, _ = place(chips)
     zs, z, y = chips // 2, chip // 2, chip % 2
     hops = zs // 2
@@ -221,8 +205,9 @@
     def arrive(stream, step):
         k, way, _, yy = stream
         n = k * hops + step - 1
-        block = spot(z - way * step, yy)
-        remote(block, block, ssem.at[n], rsem.at[n], {"row": line(zs, z, y, core)}).wait_recv()
+        where = ((z - way * step + zs) % zs) * 2 + yy
+        remote(at(where), at(where), ssem.at[n], rsem.at[n], {"row": line(zs, z, y, core)}).wait_recv()
+        return where
 
     across = {"row": line(zs, z, 1 - y, core)}
     swap = remote(spot(z, y), spot(z, y), ysem.at[2], ysem.at[3], across)
@@ -235,53 +220,103 @@
     for st in order[2:]:
         if st[2]:
             send(st, 1)
+    landed(z * 2 + y)
+    landed(z * 2 + 1 - y)
     for step in range(1, hops + 1):
         for st in order:
             if step <= st[2]:
-                arrive(st, step)
+                where = arrive(st, step)
                 if step < st[2]:
                     send(st, step + 1)
+                landed(where)
     swap.wait_send()
     for copy in sent:
         copy.wait_send()
 
 
-def square_kernel(chips, in_ref, out_ref, sib_buf, half, slots, core_s, core_r, a_s, a_r, b_s, b_r):
+def square_kernel(chips, delta_hbm, sketch_hbm, x_ref, out_ref, delta, sketch, term, sib_buf, half,
+                  slots, load_s, core_s, core_r, a_s, a_r, b_s, b_r):
     chip, core, sib = place(chips)
-    greet(chips, 0, True)
-    swap = remote(in_ref.at[1 - core], sib_buf, core_s.at[0], core_r.at[0], {"row": sib})
+    hello(chips, 0)
+    n = x_ref.shape[1]
+    part = slots.shape[1]
+    side = chips * part
+    loads = []
+    deep = delta.shape[1] // LOADS
+    for i in range(LOADS):
+        at = slice(i * deep, (i + 1) * deep)
+        loads.append((
+            pltpu.make_async_copy(delta_hbm.at[:, at], delta.at[:, at], load_s.at[2 * i]),
+            pltpu.make_async_copy(sketch_hbm.at[at], sketch.at[at], load_s.at[2 * i + 1]),
+        ))
+        for copy in loads[-1]:
+            copy.start()
+    for i in range(LOADS):
+        for copy in loads[i]:
+            copy.wait()
+        at = slice(i * deep, (i + 1) * deep)
+        product = jnp.dot(delta[:, at], sketch[at], preferred_element_type=f32)
+        x_ref[...] = x_ref[...] + product if i else product
+    across = x_ref[...].T
+    top = 0
+    for at in range(0, n, 128):
+        wide = min(128, n - at)
+        piece = dot_nn(across[at:], x_ref[:, at:at + wide])
+        if wide < 128:
+            piece = jnp.concatenate([piece, jnp.zeros((n - at, 128 - wide), f32)], axis=1)
+        term[top:top + n - at] = piece
+        top += n - at
+    if top < 2 * side:
+        term[top:] = jnp.zeros((2 * side - top, 128), f32)
+    barrier_wait(chips, 1)
+
+    def of_side(which):
+        return pl.ds(pl.multiple_of(which * side, part), side)
+
+    def of_chip(ref, at):
+        return ref.at[pl.ds(pl.multiple_of(at * part, part), part)]
+
+    swap = remote(term.at[of_side(1 - core)], sib_buf, core_s.at[0], core_r.at[0], {"row": sib})
     swap.start()
     swap.wait()
-    half[...] = in_ref[core] + sib_buf[...]
-    src, dst = (lambda c: half.at[c]), (lambda d: slots.at[d])
+    half[...] = term[of_side(core)] + sib_buf[...]
+    src, dst = (lambda c: of_chip(half, c)), (lambda d: slots.at[d])
     to_chips(chips, src, dst, a_s, a_r)
     wait_chips(chips, src, dst, a_s, a_r)
-    total = lax.fori_loop(1, chips, lambda d, t: t + slots[d], half[chip])
-    out_ref[core, chip] = total
-    src = lambda c: out_ref.at[core, chip]
-    to_chips(chips, src, lambda d: out_ref.at[core, chip], b_s, b_r)
-    wait_chips(chips, src, lambda d: out_ref.at[core, around(chip, chips - d, chips)], b_s, b_r)
-    swap = remote(out_ref.at[core], out_ref.at[core], core_s.at[1], core_r.at[1], {"row": sib})
+    own = pl.ds(pl.multiple_of(chip * part, part), part)
+    total = lax.fori_loop(1, chips, lambda d, t: t + slots[d], half[own])
+    out_ref[pl.ds(pl.multiple_of((core * chips + chip) * part, part), part)] = total
+    src = lambda c: of_chip(out_ref, core * chips + chip)
+    to_chips(chips, src, lambda d: src(0), b_s, b_r)
+    wait_chips(chips, src, lambda d: of_chip(out_ref, core * chips + around(chip, chips - d, chips)),
+               b_s, b_r)
+    mine, theirs = out_ref.at[of_side(core)], out_ref.at[of_side(1 - core)]
+    swap = remote(mine, mine, core_s.at[1], core_r.at[1], {"row": sib})
     swap.start()
     swap.wait_send()
-    remote(out_ref.at[core], out_ref.at[1 - core], core_s.at[1], core_r.at[1], {"row": sib}).wait_recv()
-
-
-def all_reduce_square(packed, chips):
-    rows, lanes = packed.shape
-    part = rows // (2 * chips)
-    shaped = packed.reshape(2, chips, part, lanes)
-    out = pl.pallas_call(
+    remote(mine, theirs, core_s.at[1], core_r.at[1], {"row": sib}).wait_recv()
+
+
+def sketch_and_square(delta, sketch, chips):
+    rows, features = delta.shape
+    n = sketch.shape[1]
+    packed = sum(n - at for at in range(0, n, 128))
+    part = -(-packed // (16 * chips)) * 8
+    anywhere = pl.BlockSpec(memory_space=pl.ANY)
+    return pl.pallas_call(
         functools.partial(square_kernel, chips),
-        out_shape=jax.ShapeDtypeStruct(shaped.shape, f32),
-        in_specs=[VMEM],
-        out_specs=VMEM,
-        scratch_shapes=[pltpu.VMEM((chips, part, lanes), f32)] * 3
-        + [DMA((2,)), DMA((2,))] + [DMA((chips,))] * 4,
+        out_shape=(jax.ShapeDtypeStruct((rows, n), f32),
+                   jax.ShapeDtypeStruct((2 * chips * part, 128), f32)),
+        in_specs=[anywhere, anywhere],
+        out_specs=(VMEM, VMEM),
+        scratch_shapes=[pltpu.VMEM(delta.shape, bf16), pltpu.VMEM(sketch.shape, bf16),
+                        pltpu.VMEM((2 * chips * part, 128), f32)]
+        + [pltpu.VMEM((chips * part, 128), f32)] * 2
+        + [pltpu.VMEM((chips, part, 128), f32), DMA((2 * LOADS,)), DMA((2,)), DMA((2,))]
+        + [DMA((chips,))] * 4,
         compiler_params=params(1),
         name="square_sum",
-    )(shaped)
-    return out.reshape(rows, lanes)
+    )(delta, sketch)
 
 
 def dot_nt(a, b):
@@ -444,8 +479,8 @@
     chips, tasks, own_ref, delta_hbm, out_ref, wall_ref,
     delta, turned, stack, packed, terms, sib_buf, half, slots, column, matrix, final,
     slab, slab2, slab3, parts, sib_parts, half2, slots2, other, other_in, mine, block, gathered, wpacked,
-    local_s, g_s, g_r, sw_s, sw_r, core_s, core_r, a_s, a_r, b_s, b_r, c_s, c_r,
-    t1_s, t1_r, t2_s, t2_r, t3_s, t3_r, w_s, w_r, sp_s, sp_r, d_s, d_r, e_s, e_r, y_sem, t4_s, t4_r,
+    local_s, g_s, g_r, sw_s, sw_r, a_s, a_r, b_s, b_r, c_s, c_r, p_s, p_r, q_s, q_r,
+    t1_s, t1_r, t2_s, t2_r, t3_s, t3_r, w_s, w_r, sp_s, sp_r, d_s, d_r, e_s, e_r, y_sem, t4_s, t4_r, f_s, f_r,
 ):
     chip, core, sib = place(chips)
     me = lax.axis_index("task")
@@ -503,28 +538,48 @@
     tsrc = lambda c: slab.at[me]
     start_tasks(tasks, tsrc, lambda c: slab.at[c], t1_s, t1_r)
 
-    def gather(buf, sems, recvs, n, beside):
-        mine_at = lambda c: buf.at[chip, core]
-        to_chips(chips, mine_at, lambda d: buf.at[chip, core], sems, recvs)
-        beside()
-        wait_chips(chips, mine_at, lambda d: buf.at[around(chip, chips - d, chips), core], sems, recvs)
-        swap = remote(buf.at[:, core], buf.at[:, core], core_s.at[n], core_r.at[n], {"row": sib})
-        swap.start()
-        swap.wait_send()
-        remote(buf.at[:, core], buf.at[:, 1 - core], core_s.at[n], core_r.at[n],
-               {"row": sib}).wait_recv()
-
-    span = turned.shape[0] // tasks
-
-    def turn():
-        load.wait()
-        loop(0, tasks, lambda u: turned.__setitem__(
-            pl.ds(pl.multiple_of(u * span, span), span),
-            delta[:, pl.ds(pl.multiple_of(u * span, span), span)].T))
-
-    gather(column, b_s, b_r, 1, turn)
-    loop(0, chips * 2, lambda i: unpack_to(
-        matrix.at[i], column[i // 2, i % 2], depth, width))
+    span = turned.shape[0] // (2 * chips)
+
+    def turn(i):
+        at = pl.ds(pl.multiple_of(i * span, span), span)
+        turned[at] = delta[:, at].T
+
+    def gather(buf, sems, recvs, ps, pr, number):
+        def spot(c, which):
+            return buf.at[c, which]
+
+        def pass_on(c):
+            return remote(spot(c, core), spot(c, core), ps.at[c], pr.at[c], {"row": sib})
+
+        def place_in(c, which):
+            unpack_to(matrix.at[c * 2 + which], buf[c, which], depth, width)
+
+        to_chips(chips, lambda c: spot(chip, core), lambda d: spot(chip, core), sems, recvs)
+        pass_on(chip).start()
+        place_in(chip, core)
+        turn(number * chips)
+
+        def arrival(d):
+            turn(number * chips + d)
+            c = around(chip, chips - d, chips)
+            remote(spot(c, core), spot(c, core), sems.at[d], recvs.at[d], {"row": sib}).wait_recv()
+            pass_on(c).start()
+            place_in(c, core)
+
+        loop(1, chips, arrival)
+
+        def other_core(d):
+            c = around(chip, chips - d, chips)
+            remote(spot(c, core), spot(c, 1 - core), ps.at[c], pr.at[c], {"row": sib}).wait_recv()
+            place_in(c, 1 - core)
+
+        loop(0, chips, other_core)
+        loop(0, chips, lambda c: pass_on(c).wait_send())
+        loop(1, chips, lambda d: remote(
+            spot(chip, core), spot(chip, core), sems.at[d], recvs.at[d], {"row": sib}).wait_send())
+
+    load.wait()
+    gather(column, b_s, b_r, p_s, p_r, 0)
     wait_tasks(tasks, tsrc, lambda c: slab.at[c], t1_s, t1_r)
 
     def times(left):
@@ -546,9 +601,7 @@
     part = -2.4375 * gram + 1.6875 * two - 0.5625 * three
     wait_tasks(tasks, src3, lambda c: slab3.at[c], t3_s, t3_r)
     final[chip, core] = (part + 0.0625 * pack_rows(times(slab3))).astype(bf16)
-    gather(final, c_s, c_r, 2, lambda: None)
-    loop(0, chips * 2, lambda i: unpack_to(
-        matrix.at[i], final[i // 2, i % 2], depth, width))
+    gather(final, c_s, c_r, q_s, q_r, 1)
 
     def apply(s, total):
         right = matrix[pl.ds(s * per, per)].reshape(width, width)
@@ -564,7 +617,8 @@
         return remote(parts.at[u, :, 1 - core], sib_parts.at[u], sp_s.at[u], sp_r.at[u], {"row": sib})
 
     def coef_term(u):
-        rows_u = turned[pl.ds(pl.multiple_of(u * span, span), span)]
+        tall = turned.shape[0] // tasks
+        rows_u = turned[pl.ds(pl.multiple_of(u * tall, tall), tall)]
         term = jnp.dot(rows_u, wall_ref[me], preferred_element_type=f32).astype(bf16)
         parts[u] = term.reshape(parts.shape[1:])
         swap_part(u).start()
@@ -593,22 +647,28 @@
     wait_tasks(tasks, tsrc4, tdst4, t4_s, t4_r)
     for p in range(pairs):
         gathered[core, chip, p] = pack_pair(block[2 * p], block[2 * p + 1])
-    ring_gather(chips, lambda c: gathered.at[core, c], e_s, e_r, y_sem)
-    swap = remote(gathered.at[core], gathered.at[core], core_s.at[0], core_r.at[0], {"row": sib})
-    swap.start()
-
-    def spill(which):
-        def body(c):
-            for p in range(pairs):
-                for v, piece in enumerate(unpack_pair(gathered[which, c, p], width)):
-                    out_ref[2 * p + v, c, which] = piece
-        loop(0, chips, body)
-
-    spill(core)
-    swap.wait_send()
-    remote(gathered.at[core], gathered.at[1 - core], core_s.at[0], core_r.at[0],
-           {"row": sib}).wait_recv()
-    spill(1 - core)
+    seen = []
+
+    def spill(c, which):
+        for p in range(pairs):
+            for v, piece in enumerate(unpack_pair(gathered[which, c, p], width)):
+                out_ref[2 * p + v, c, which] = piece
+
+    def pass_on(c):
+        spot = gathered.at[core, c]
+        return remote(spot, spot, f_s.at[c], f_r.at[c], {"row": sib})
+
+    def landed(c):
+        pass_on(c).start()
+        seen.append(c)
+        spill(c, core)
+
+    ring_gather(chips, lambda c: gathered.at[core, c], e_s, e_r, y_sem, landed)
+    for c in seen:
+        remote(gathered.at[core, c], gathered.at[1 - core, c], f_s.at[c], f_r.at[c],
+               {"row": sib}).wait_recv()
+        spill(c, 1 - core)
+    loop(0, chips, lambda c: pass_on(c).wait_send())
 
 
 def joint(own, delta, chips, tasks):
@@ -637,20 +697,11 @@
             buf(chips, *chunk), buf(chips, *chunk), buf(*chunk), buf(*chunk),
             buf(tasks, piece, width), buf(tasks, piece, width), buf(2, chips, *chunk),
             buf(tasks, tall, 128), DMA((1,)),
-        ] + pair(tasks) + pair(tasks) + pair(3) + pair(chips) * 3
-        + pair(tasks) * 5 + pair(chips) * 2 + [DMA((4,))] + pair(tasks),
+        ] + pair(tasks) + pair(tasks) + pair(chips) * 5
+        + pair(tasks) * 5 + pair(chips) * 2 + [DMA((4,))] + pair(tasks) + pair(chips),
         compiler_params=params(2),
         name="joint",
     )(own, delta)
-
-
-def pack(square):
-    n = square.shape[0]
-    parts = []
-    for at in range(0, n, 128):
-        piece = square[at:, at:min(at + 128, n)]
-        parts.append(jnp.pad(piece, ((0, 0), (0, 128 - piece.shape[1]))))
-    return jnp.concatenate(parts, axis=0)
 
 
 def local(delta, sketch, base):
@@ -658,11 +709,7 @@
     chips = lax.axis_size("row") // 2
     delta_rows, task_sketch = delta[0], sketch[0]
     width = task_sketch.shape[1]
-    sketched = jnp.dot(delta_rows, task_sketch, preferred_element_type=f32)
-    packed = pack(jnp.dot(sketched.T, sketched, precision=highest))
-    unit = 16 * chips
-    packed = jnp.pad(packed, ((0, -packed.shape[0] % unit), (0, 0)))
-    packed = all_reduce_square(packed, chips)
+    sketched, packed = sketch_and_square(delta_rows, task_sketch, chips)
     own = basis_of(packed, sketched, 1.0 / math.sqrt(tasks))
     coefs, stack = joint(own, delta_rows, chips, tasks)
     coefs = coefs.reshape(tasks, -1, width)

time: 261 us -> 245 us (0.939)
  Pallas kernels: 244 us -> 237 us
  matrix products: 9.82 us -> 4.28 us
  local copies, waits for them, and re-layouts: 6.52 us -> 3.32 us
    pallas_call x1, Pallas kernels: 199 us -> 193 us  [joint(): pl.pallas_call(functools.partial(joint_kernel, chips, tasks), out_shape=(...]
    dot_general x2 -> x0, matrix products: 5.54 us -> none  [the longest x1 3.57 us: local(): sketched = jnp.dot(delta_rows, task_sketch, preferred_element_type=f32)]
where the time goes in v4:
time: 245 us
  Pallas kernels  237 us (97%)
  matrix products  4.28 us (2%)
  local copies, waits for them, and re-layouts  3.32 us (1%)
    pallas_call x1, Pallas kernels, joint(): pl.pallas_call(functools.partial(joint_kernel, chips, tasks), out_shape=(...  193 us
    pallas_call x1, Pallas kernels, sketch_and_square(): pl.pallas_call(functools.partial(square_kernel, chips), out_shape=(jax.Sh...  30.5 us
    pallas_call x1, Pallas kernels, basis_of(): pl.pallas_call(functools.partial(basis_kernel, shrink), out_shape=jax.Sha...  13.5 us

profile of v4, /device:TPU:1, one launch (start us, length us, event | category | flops | bytes accessed | tf_op | source)
XLA Modules:
  0.0 245.0 jit_solution(2466418223879637253)
XLA Ops:
  0.0 3.3 %copy.4 = bf16[1,4096,320]{2,1,0:T(8,128)(2,1)S(1)} copy(bf16[1,4096,320]{1,2,0:T(8,128)(2,1)} %param.4) | data formatting | bytes 5242880 | tf_op args[1]
  3.3 30.5 %square_sum.1 = (f32[448,320]{1,0:T(8,128)S(1)}, f32[768,128]{1,0:T(8,128)S(1)}) custom-call(bf16[448,4096]{1,0:T(8,128)(2,1)} %bitcast.12, bf16[4096,320]{1,0:T(8,128)(2,1)S(1)} %bitcast.11), custom_call_target="tpu_custom_call" | custom-call | tf_op jit(solution)/shard_map/square_sum/pallas_call | solution.py:306
  33.9 0.0 copy-start
  33.9 13.5 %basis.1.own_ref = f32[448,320]{1,0:T(8,128)S(1)} custom-call(f32[768,128]{1,0:T(8,128)S(1)} %get-tuple-element.9.packed, f32[448,320]{1,0:T(8,128)S(1)} %get-tuple-element.10.x_ref), custom_call_target="tpu_custom_call" | custom-call | tf_op jit(solution)/shard_map/basis/pallas_call | solution.py:376
  47.3 193.4 %joint.1 = (bf16[8,16,2,16,320]{4,3,2,1,0:T(8,128)(2,1)}, bf16[8,448,320]{2,1,0:T(8,128)(2,1)S(1)}) custom-call(f32[448,320]{1,0:T(8,128)S(1)} %basis.1.own_ref, bf16[448,4096]{1,0:T(8,128)(2,1)} %bitcast.13), custom_call_target="tpu_custom_call" | custom-call | tf_op jit(solution)/shard_map/joint/pallas_call | solution.py:684
  240.7 0.0 copy-done
  240.7 4.3 %fusion.1 = bf16[448,512]{1,0:T(8,128)(2,1)} fusion(bf16[8,448,320]{2,1,0:T(8,128)(2,1)S(1)} %get-tuple-element.11, bf16[8,512,320]{2,1,0:T(8,128)(2,1)} %bitcast.14, bf16[448,512]{1,0:T(8,128)(2,1)S(1)} %copy-done), kind=kOutput, calls=%fused_computation.2 | convolution fusion | flops 1175093248 | bytes 5832704 | tf_op jit(solution)/shard_map/dot_general | solution.py:716
Async XLA Ops:
  33.9 206.8 %copy-start = (bf16[448,512]{1,0:T(8,128)(2,1)S(1)}, bf16[448,512]{1,0:T(8,128)(2,1)}, u32[]{:S(2)}) copy-start(bf16[448,512]{1,0:T(8,128)(2,1)} %param.5) | copy-start | bytes 1376260

commit v5 on v4

--- a/solution.py
+++ b/solution.py
@@ -185,7 +185,7 @@
     return own + other_in[...].astype(f32)
 
 
-def ring_gather(chips, at, ssem, rsem, ysem, landed):
+def ring_gather(chips, at, ssem, rsem, ysem, landed, between=lambda step: None):
     chip, core, _ = place(chips)
     zs, z, y = chips // 2, chip // 2, chip % 2
     hops = zs // 2
@@ -229,6 +229,7 @@
                 if step < st[2]:
                     send(st, step + 1)
                 landed(where)
+        between(step)
     swap.wait_send()
     for copy in sent:
         copy.wait_send()
@@ -247,7 +248,7 @@
         at = slice(i * deep, (i + 1) * deep)
         loads.append((
             pltpu.make_async_copy(delta_hbm.at[:, at], delta.at[:, at], load_s.at[2 * i]),
-            pltpu.make_async_copy(sketch_hbm.at[at], sketch.at[at], load_s.at[2 * i + 1]),
+            pltpu.make_async_copy(sketch_hbm.at[:, at], sketch.at[:, at], load_s.at[2 * i + 1]),
         ))
         for copy in loads[-1]:
             copy.start()
@@ -255,7 +256,8 @@
         for copy in loads[i]:
             copy.wait()
         at = slice(i * deep, (i + 1) * deep)
-        product = jnp.dot(delta[:, at], sketch[at], preferred_element_type=f32)
+        product = lax.dot_general(delta[:, at], sketch[:, at], (((1,), (1,)), ((), ())),
+                                  preferred_element_type=f32)
         x_ref[...] = x_ref[...] + product if i else product
     across = x_ref[...].T
     top = 0
@@ -299,7 +301,7 @@
 
 def sketch_and_square(delta, sketch, chips):
     rows, features = delta.shape
-    n = sketch.shape[1]
+    n = sketch.shape[0]
     packed = sum(n - at for at in range(0, n, 128))
     part = -(-packed // (16 * chips)) * 8
     anywhere = pl.BlockSpec(memory_space=pl.ANY)
@@ -479,7 +481,7 @@
     chips, tasks, own_ref, delta_hbm, out_ref, wall_ref,
     delta, turned, stack, packed, terms, sib_buf, half, slots, column, matrix, final,
     slab, slab2, slab3, parts, sib_parts, half2, slots2, other, other_in, mine, block, gathered, wpacked,
-    local_s, g_s, g_r, sw_s, sw_r, a_s, a_r, b_s, b_r, c_s, c_r, p_s, p_r, q_s, q_r,
+    local_s, g_s, g_r, sw_s, sw_r, a_s, a_r, b_s, b_r, c_s, c_r, power, total_w, y1_s, y2_s, p_s, p_r, q_s, q_r,
     t1_s, t1_r, t2_s, t2_r, t3_s, t3_r, w_s, w_r, sp_s, sp_r, d_s, d_r, e_s, e_r, y_sem, t4_s, t4_r, f_s, f_r,
 ):
     chip, core, sib = place(chips)
@@ -518,6 +520,17 @@
             def _():
                 remote(half.at[c], slots.at[d], a_s.at[d], a_r.at[d], {"row": c * 2 + core}).start()
 
+    load.wait()
+    span = turned.shape[0] // (2 * chips)
+    turned_count = [0]
+
+    def turns(n):
+        for _ in range(n):
+            i = turned_count[0]
+            if i < 2 * chips:
+                turned[i * span:(i + 1) * span] = delta[:, i * span:(i + 1) * span].T
+                turned_count[0] += 1
+
     steps = spread(tasks, lambda c: packed.at[c], g_s, g_r)
     next(steps)
     gram_term(me, 0)
@@ -526,6 +539,7 @@
         unpack_to(stack.at[got], packed[got], rows, width)
         ready.append(got)
         gram_term(got, len(ready) - 1)
+        turns(2)
         to_owner(ready[-2], len(ready) - 2)
     to_owner(ready[-1], len(ready) - 1)
     wait_chips(chips, lambda c: half.at[c], lambda d: slots.at[d], a_s, a_r)
@@ -533,81 +547,96 @@
         1, chips, lambda d, t: t + slots[d].astype(f32), half[chip].astype(f32))
     first = gram.astype(bf16)
     slab[me] = first
-    column[chip, core] = first
 
     tsrc = lambda c: slab.at[me]
     start_tasks(tasks, tsrc, lambda c: slab.at[c], t1_s, t1_r)
 
-    span = turned.shape[0] // (2 * chips)
-
-    def turn(i):
-        at = pl.ds(pl.multiple_of(i * span, span), span)
-        turned[at] = delta[:, at].T
-
-    def gather(buf, sems, recvs, ps, pr, number):
-        def spot(c, which):
-            return buf.at[c, which]
+    def gather(buf, sems, recvs, ys, ps, pr, prepare, use):
+        seen, used = [], []
 
         def pass_on(c):
-            return remote(spot(c, core), spot(c, core), ps.at[c], pr.at[c], {"row": sib})
-
-        def place_in(c, which):
-            unpack_to(matrix.at[c * 2 + which], buf[c, which], depth, width)
-
-        to_chips(chips, lambda c: spot(chip, core), lambda d: spot(chip, core), sems, recvs)
-        pass_on(chip).start()
-        place_in(chip, core)
-        turn(number * chips)
-
-        def arrival(d):
-            turn(number * chips + d)
-            c = around(chip, chips - d, chips)
-            remote(spot(c, core), spot(c, core), sems.at[d], recvs.at[d], {"row": sib}).wait_recv()
+            return remote(buf.at[c, core], buf.at[c, core], ps.at[c], pr.at[c], {"row": sib})
+
+        def landed(c):
             pass_on(c).start()
-            place_in(c, core)
-
-        loop(1, chips, arrival)
-
-        def other_core(d):
-            c = around(chip, chips - d, chips)
-            remote(spot(c, core), spot(c, 1 - core), ps.at[c], pr.at[c], {"row": sib}).wait_recv()
-            place_in(c, 1 - core)
-
-        loop(0, chips, other_core)
+            seen.append(c)
+            unpack_to(matrix.at[c * 2 + core], buf[c, core], depth, width)
+
+        def finish(upto):
+            for c in seen[len(used):upto]:
+                remote(buf.at[c, core], buf.at[c, 1 - core], ps.at[c], pr.at[c], {"row": sib}).wait_recv()
+                unpack_to(matrix.at[c * 2 + 1 - core], buf[c, 1 - core], depth, width)
+                used.append(c)
+
+        def between(step):
+            if step == 1:
+                prepare()
+            finish(2 + 4 * (step - 1))
+            whole()
+            turns(1)
+
+        tasks_used = []
+
+        def whole():
+            if per != 4:
+                return
+            zs, z = chips // 2, chip // 2
+            order = [0]
+            for step in range(1, zs // 2):
+                order += [-step, step]
+            order += [zs // 2]
+            for n, off in enumerate(order):
+                needs = 2 if n == 0 else 2 + 4 * ((n + 1) // 2)
+                if n == len(order) - 1:
+                    needs = chips
+                if n not in tasks_used and len(used) >= needs:
+                    tasks_used.append(n)
+                    use((z + off + zs) % zs)
+
+        ring_gather(chips, lambda c: buf.at[c, core], sems, recvs, ys, landed, between)
+        finish(chips)
+        whole()
+        if per != 4:
+            loop(0, tasks, use)
         loop(0, chips, lambda c: pass_on(c).wait_send())
-        loop(1, chips, lambda d: remote(
-            spot(chip, core), spot(chip, core), sems.at[d], recvs.at[d], {"row": sib}).wait_send())
-
-    load.wait()
-    gather(column, b_s, b_r, p_s, p_r, 0)
-    wait_tasks(tasks, tsrc, lambda c: slab.at[c], t1_s, t1_r)
+
+    def times_one(left, s):
+        right = matrix[pl.ds(s * per, per)].reshape(width, width)
+        return jnp.dot(unpack_rows(left[s], depth, width), right, preferred_element_type=f32)
+
+    def square_one(s):
+        power[...] += times_one(slab, s)
 
     def times(left):
-        def body(s, total):
-            right = matrix[pl.ds(s * per, per)].reshape(width, width)
-            return total + jnp.dot(
-                unpack_rows(left[s], depth, width), right, preferred_element_type=f32)
-        return lax.fori_loop(0, tasks, body, jnp.zeros((depth, width), f32))
-
-    two = pack_rows(times(slab))
+        return lax.fori_loop(
+            0, tasks, lambda s, total: total + times_one(left, s), jnp.zeros((depth, width), f32))
+
+    power[...] = jnp.zeros_like(power)
+    column[chip, core] = first
+    gather(column, b_s, b_r, y1_s, p_s, p_r,
+           lambda: wait_tasks(tasks, tsrc, lambda c: slab.at[c], t1_s, t1_r), square_one)
+    two = pack_rows(power[...])
     slab2[me] = two.astype(bf16)
     src2 = lambda c: slab2.at[me]
     start_tasks(tasks, src2, lambda c: slab2.at[c], t2_s, t2_r)
+    turns(5)
     wait_tasks(tasks, src2, lambda c: slab2.at[c], t2_s, t2_r)
     three = pack_rows(times(slab2))
     slab3[me] = three.astype(bf16)
     src3 = lambda c: slab3.at[me]
     start_tasks(tasks, src3, lambda c: slab3.at[c], t3_s, t3_r)
     part = -2.4375 * gram + 1.6875 * two - 0.5625 * three
+    turns(5)
     wait_tasks(tasks, src3, lambda c: slab3.at[c], t3_s, t3_r)
     final[chip, core] = (part + 0.0625 * pack_rows(times(slab3))).astype(bf16)
-    gather(final, c_s, c_r, q_s, q_r, 1)
-
-    def apply(s, total):
+
+    def apply(s):
         right = matrix[pl.ds(s * per, per)].reshape(width, width)
-        return total + jnp.dot(stack[s], right, preferred_element_type=f32)
-
-    weights = lax.fori_loop(0, tasks, apply, 2.25 * own_ref[...]).astype(bf16)
+        total_w[...] += jnp.dot(stack[s], right, preferred_element_type=f32)
+
+    total_w[...] = 2.25 * own_ref[...]
+    gather(final, c_s, c_r, y2_s, q_s, q_r, lambda: None, apply)
+    weights = total_w[...].astype(bf16)
     wall_ref[me] = weights
     wpacked[me] = pack_rows(weights)
     wsteps = spread(tasks, lambda c: wpacked.at[c], w_s, w_r)
@@ -623,6 +652,7 @@
         parts[u] = term.reshape(parts.shape[1:])
         swap_part(u).start()
 
+    turns(2 * chips)
     loop(0, tasks, coef_term)
     loop(0, tasks, lambda u: swap_part(u).wait())
 
@@ -697,7 +727,9 @@
             buf(chips, *chunk), buf(chips, *chunk), buf(*chunk), buf(*chunk),
             buf(tasks, piece, width), buf(tasks, piece, width), buf(2, chips, *chunk),
             buf(tasks, tall, 128), DMA((1,)),
-        ] + pair(tasks) + pair(tasks) + pair(chips) * 5
+        ] + pair(tasks) + pair(tasks) + pair(chips) * 3
+        + [pltpu.VMEM((depth, width), f32), pltpu.VMEM((rows, width), f32), DMA((4,)), DMA((4,))]
+        + pair(chips) * 2
         + pair(tasks) * 5 + pair(chips) * 2 + [DMA((4,))] + pair(tasks) + pair(chips),
         compiler_params=params(2),
         name="joint",
@@ -709,7 +741,7 @@
     chips = lax.axis_size("row") // 2
     delta_rows, task_sketch = delta[0], sketch[0]
     width = task_sketch.shape[1]
-    sketched, packed = sketch_and_square(delta_rows, task_sketch, chips)
+    sketched, packed = sketch_and_square(delta_rows, task_sketch.T, chips)
     own = basis_of(packed, sketched, 1.0 / math.sqrt(tasks))
     coefs, stack = joint(own, delta_rows, chips, tasks)
     coefs = coefs.reshape(tasks, -1, width)

time: 245 us -> 223 us (0.910)
  Pallas kernels: 237 us -> 217 us
    pallas_call x1, Pallas kernels: 193 us -> 172 us  [joint(): pl.pallas_call(functools.partial(joint_kernel, chips, tasks), out_shape=(...]
where the time goes in v5:
time: 223 us
  Pallas kernels  217 us (97%)
  matrix products  4.28 us (2%)
    pallas_call x1, Pallas kernels, joint(): pl.pallas_call(functools.partial(joint_kernel, chips, tasks), out_shape=(...  172 us
    pallas_call x1, Pallas kernels, sketch_and_square(): pl.pallas_call(functools.partial(square_kernel, chips), out_shape=(jax.Sh...  31.4 us
    pallas_call x1, Pallas kernels, basis_of(): pl.pallas_call(functools.partial(basis_kernel, shrink), out_shape=jax.Sha...  13.5 us

profile of v5, /device:TPU:1, one launch (start us, length us, event | category | flops | bytes accessed | tf_op | source)
XLA Modules:
  0.0 222.8 jit_solution(2897754670179629063)
XLA Ops:
  0.0 0.0 copy-start
  0.0 1.7 copy-done
  1.7 31.4 %square_sum.1 = (f32[448,320]{1,0:T(8,128)S(1)}, f32[768,128]{1,0:T(8,128)S(1)}) custom-call(bf16[448,4096]{1,0:T(8,128)(2,1)} %bitcast.14, bf16[320,4096]{1,0:T(8,128)(2,1)S(1)} %bitcast.13), custom_call_target="tpu_custom_call" | custom-call | tf_op jit(solution)/shard_map/square_sum/pallas_call | solution.py:308
  33.2 0.0 copy-start.1
  33.2 13.5 %basis.1.own_ref = f32[448,320]{1,0:T(8,128)S(1)} custom-call(f32[768,128]{1,0:T(8,128)S(1)} %get-tuple-element.9.packed, f32[448,320]{1,0:T(8,128)S(1)} %get-tuple-element.10.x_ref), custom_call_target="tpu_custom_call" | custom-call | tf_op jit(solution)/shard_map/basis/pallas_call | solution.py:378
  46.6 171.8 %joint.1 = (bf16[8,16,2,16,320]{4,3,2,1,0:T(8,128)(2,1)}, bf16[8,448,320]{2,1,0:T(8,128)(2,1)S(1)}) custom-call(f32[448,320]{1,0:T(8,128)S(1)} %basis.1.own_ref, bf16[448,4096]{1,0:T(8,128)(2,1)} %bitcast.15), custom_call_target="tpu_custom_call" | custom-call | tf_op jit(solution)/shard_map/joint/pallas_call | solution.py:714
  218.5 0.0 copy-done.1
  218.5 4.3 %fusion.1 = bf16[448,512]{1,0:T(8,128)(2,1)} fusion(bf16[8,448,320]{2,1,0:T(8,128)(2,1)S(1)} %get-tuple-element.11, bf16[8,512,320]{2,1,0:T(8,128)(2,1)} %bitcast.16, bf16[448,512]{1,0:T(8,128)(2,1)S(1)} %copy-done.1), kind=kOutput, calls=%fused_computation.2 | convolution fusion | flops 1175093248 | bytes 5832704 | tf_op jit(solution)/shard_map/dot_general | solution.py:748
Async XLA Ops:
  0.0 1.7 copy-start
  33.2 185.3 %copy-start.1 = (bf16[448,512]{1,0:T(8,128)(2,1)S(1)}, bf16[448,512]{1,0:T(8,128)(2,1)}, u32[]{:S(2)}) copy-start(bf16[448,512]{1,0:T(8,128)(2,1)} %param.5) | copy-start | bytes 1376260

commit v6 on v5

--- a/solution.py
+++ b/solution.py
@@ -21,7 +21,7 @@
 
 def params(cid):
     return pltpu.CompilerParams(
-        collective_id=cid, has_side_effects=True, vmem_limit_bytes=48 * 1024 * 1024
+        collective_id=cid, has_side_effects=True, vmem_limit_bytes=56 * 1024 * 1024
     )
 
 
@@ -134,7 +134,7 @@
     return [(2, 1, near, 1 - y), (3, -1, far, 1 - y), (0, 1, far, y), (1, -1, near, y)]
 
 
-def ring_reduce(chips, half, slots, other, other_in, ssem, rsem, ysem):
+def ring_reduce(chips, half, slots, other, other_in, ssem, rsem, ysem, between):
     chip, core, _ = place(chips)
     zs, z, y = chips // 2, chip // 2, chip % 2
     hops = zs // 2
@@ -167,6 +167,7 @@
                     dest = z + st[1] * (st[2] - step)
                     slots[n] = (slots[n].astype(f32) + term(dest, st[3]).astype(f32)).astype(bf16)
                     send(st, step + 1, slots.at[n])
+        between()
 
     def final(plane, pair):
         total = term(z, plane).astype(f32)
@@ -223,22 +224,24 @@
     landed(z * 2 + y)
     landed(z * 2 + 1 - y)
     for step in range(1, hops + 1):
+        new = []
         for st in order:
             if step <= st[2]:
-                where = arrive(st, step)
+                new.append(arrive(st, step))
                 if step < st[2]:
                     send(st, step + 1)
-                landed(where)
+        for where in new:
+            landed(where)
         between(step)
     swap.wait_send()
     for copy in sent:
         copy.wait_send()
 
 
-def square_kernel(chips, delta_hbm, sketch_hbm, x_ref, out_ref, delta, sketch, term, sib_buf, half,
-                  slots, load_s, core_s, core_r, a_s, a_r, b_s, b_r):
+def square_stage(chips, tasks, turns, delta_hbm, sketch_hbm, x_ref, out_ref, delta, sketch, term,
+                 sib_buf, half, slots, load_s, core_s, core_r, a_s, a_r, b_s, b_r):
     chip, core, sib = place(chips)
-    hello(chips, 0)
+    hello(chips, tasks)
     n = x_ref.shape[1]
     part = slots.shape[1]
     side = chips * part
@@ -270,7 +273,8 @@
         top += n - at
     if top < 2 * side:
         term[top:] = jnp.zeros((2 * side - top, 128), f32)
-    barrier_wait(chips, 1)
+    turns(4)
+    barrier_wait(chips, tasks)
 
     def of_side(which):
         return pl.ds(pl.multiple_of(which * side, part), side)
@@ -280,45 +284,38 @@
 
     swap = remote(term.at[of_side(1 - core)], sib_buf, core_s.at[0], core_r.at[0], {"row": sib})
     swap.start()
+    turns(2)
     swap.wait()
     half[...] = term[of_side(core)] + sib_buf[...]
     src, dst = (lambda c: of_chip(half, c)), (lambda d: slots.at[d])
     to_chips(chips, src, dst, a_s, a_r)
+    turns(6)
     wait_chips(chips, src, dst, a_s, a_r)
     own = pl.ds(pl.multiple_of(chip * part, part), part)
     total = lax.fori_loop(1, chips, lambda d, t: t + slots[d], half[own])
     out_ref[pl.ds(pl.multiple_of((core * chips + chip) * part, part), part)] = total
     src = lambda c: of_chip(out_ref, core * chips + chip)
     to_chips(chips, src, lambda d: src(0), b_s, b_r)
+    turns(6)
     wait_chips(chips, src, lambda d: of_chip(out_ref, core * chips + around(chip, chips - d, chips)),
                b_s, b_r)
     mine, theirs = out_ref.at[of_side(core)], out_ref.at[of_side(1 - core)]
     swap = remote(mine, mine, core_s.at[1], core_r.at[1], {"row": sib})
     swap.start()
+    turns(2)
     swap.wait_send()
     remote(mine, theirs, core_s.at[1], core_r.at[1], {"row": sib}).wait_recv()
 
 
-def sketch_and_square(delta, sketch, chips):
-    rows, features = delta.shape
+def square_scratch(delta, sketch, chips):
     n = sketch.shape[0]
     packed = sum(n - at for at in range(0, n, 128))
     part = -(-packed // (16 * chips)) * 8
-    anywhere = pl.BlockSpec(memory_space=pl.ANY)
-    return pl.pallas_call(
-        functools.partial(square_kernel, chips),
-        out_shape=(jax.ShapeDtypeStruct((rows, n), f32),
-                   jax.ShapeDtypeStruct((2 * chips * part, 128), f32)),
-        in_specs=[anywhere, anywhere],
-        out_specs=(VMEM, VMEM),
-        scratch_shapes=[pltpu.VMEM(delta.shape, bf16), pltpu.VMEM(sketch.shape, bf16),
-                        pltpu.VMEM((2 * chips * part, 128), f32)]
-        + [pltpu.VMEM((chips * part, 128), f32)] * 2
-        + [pltpu.VMEM((chips, part, 128), f32), DMA((2 * LOADS,)), DMA((2,)), DMA((2,))]
-        + [DMA((chips,))] * 4,
-        compiler_params=params(1),
-        name="square_sum",
-    )(delta, sketch)
+    return [pltpu.VMEM((delta.shape[0], n), f32), pltpu.VMEM((2 * chips * part, 128), f32),
+            pltpu.VMEM(delta.shape, bf16), pltpu.VMEM(sketch.shape, bf16),
+            pltpu.VMEM((2 * chips * part, 128), f32)] + [pltpu.VMEM((chips * part, 128), f32)] * 2 + [
+            pltpu.VMEM((chips, part, 128), f32), DMA((2 * LOADS,)), DMA((2,)), DMA((2,))
+    ] + [DMA((chips,))] * 4
 
 
 def dot_nt(a, b):
@@ -331,7 +328,7 @@
                            preferred_element_type=f32)
 
 
-def basis_kernel(shrink, packed, x_ref, own_ref, cols, fac, inv):
+def basis_stage(shrink, packed, x_ref, own_ref, cols, fac, inv):
     n = x_ref.shape[1]
     blocks = n // CB
     row_id = lax.broadcasted_iota(jnp.int32, (CB, 2 * CB), 0)
@@ -373,19 +370,6 @@
     own_ref[...] = dot_nt(x_ref[...], z) * shrink
 
 
-def basis_of(packed, sketched, shrink):
-    n = sketched.shape[1]
-    return pl.pallas_call(
-        functools.partial(basis_kernel, shrink),
-        out_shape=jax.ShapeDtypeStruct(sketched.shape, f32),
-        in_specs=[VMEM, VMEM],
-        out_specs=VMEM,
-        scratch_shapes=[pltpu.VMEM((n // CB, n, CB), f32)] * 3,
-        compiler_params=pltpu.CompilerParams(vmem_limit_bytes=32 * 1024 * 1024),
-        name="basis",
-    )(packed, sketched)
-
-
 def start_tasks(tasks, src, dst, ssem, rsem):
     me = lax.axis_index("task")
 
@@ -430,12 +414,12 @@
         send(d, own, name(x + d, y))
     yield
     twin = at(name(x, 1 - y))
-    arrive(0, twin)
-    yield name(x, 1 - y)
     across = [d for d in range(1, xs) if d == xs // 2]
     along = [d for d in range(1, xs) if d != xs // 2]
+    arrive(0, twin)
     for d in along:
         send(xs + d, twin, name(x + d, y))
+    yield name(x, 1 - y)
     for d in across:
         block = at(name(x + xs - d, y))
         arrive(d, block)
@@ -478,25 +462,36 @@
 
 
 def joint_kernel(
-    chips, tasks, own_ref, delta_hbm, out_ref, wall_ref,
-    delta, turned, stack, packed, terms, sib_buf, half, slots, column, matrix, final,
+    chips, tasks, delta_hbm, sketch_hbm, out_ref, wall_ref, square_refs, basis_refs,
+    turned, stack, packed, terms, sib_buf, half, slots, column, matrix, final,
     slab, slab2, slab3, parts, sib_parts, half2, slots2, other, other_in, mine, block, gathered, wpacked,
-    local_s, g_s, g_r, sw_s, sw_r, a_s, a_r, b_s, b_r, c_s, c_r, power, total_w, y1_s, y2_s, p_s, p_r, q_s, q_r,
+    g_s, g_r, sw_s, sw_r, a_s, a_r, b_s, b_r, c_s, c_r, power, total_w, y1_s, y2_s,
+    p_s, p_r, q_s, q_r,
     t1_s, t1_r, t2_s, t2_r, t3_s, t3_r, w_s, w_r, sp_s, sp_r, d_s, d_r, e_s, e_r, y_sem, t4_s, t4_r, f_s, f_r,
 ):
     chip, core, sib = place(chips)
     me = lax.axis_index("task")
+    x_ref, gram_ref, delta = square_refs[:3]
+    own_ref = basis_refs[0]
     rows, width = own_ref.shape
     depth = terms.shape[2]
     per = width // depth
     pairs = tasks // 2
-    hello(chips, tasks)
-    load = pltpu.make_async_copy(delta_hbm, delta, local_s.at[0])
-    load.start()
+    span = turned.shape[0] // (2 * chips)
+    turned_count = [0]
+
+    def turns(n):
+        for _ in range(n):
+            i = turned_count[0]
+            if i < 2 * chips:
+                turned[i * span:(i + 1) * span] = delta[:, i * span:(i + 1) * span].T
+                turned_count[0] += 1
+
+    square_stage(chips, tasks, turns, delta_hbm, sketch_hbm, *square_refs)
+    basis_stage(1.0 / math.sqrt(tasks), gram_ref, x_ref, *basis_refs)
     own = own_ref[...].astype(bf16)
     stack[me] = own
     packed[me] = pack_rows(own)
-    barrier_wait(chips, tasks)
 
     def swap_term(s, i):
         at = pl.ds(s * (per // 2), per // 2)
@@ -519,17 +514,6 @@
             @pl.when(c != chip)
             def _():
                 remote(half.at[c], slots.at[d], a_s.at[d], a_r.at[d], {"row": c * 2 + core}).start()
-
-    load.wait()
-    span = turned.shape[0] // (2 * chips)
-    turned_count = [0]
-
-    def turns(n):
-        for _ in range(n):
-            i = turned_count[0]
-            if i < 2 * chips:
-                turned[i * span:(i + 1) * span] = delta[:, i * span:(i + 1) * span].T
-                turned_count[0] += 1
 
     steps = spread(tasks, lambda c: packed.at[c], g_s, g_r)
     next(steps)
@@ -539,7 +523,6 @@
         unpack_to(stack.at[got], packed[got], rows, width)
         ready.append(got)
         gram_term(got, len(ready) - 1)
-        turns(2)
         to_owner(ready[-2], len(ready) - 2)
     to_owner(ready[-1], len(ready) - 1)
     wait_chips(chips, lambda c: half.at[c], lambda d: slots.at[d], a_s, a_r)
@@ -573,7 +556,6 @@
                 prepare()
             finish(2 + 4 * (step - 1))
             whole()
-            turns(1)
 
         tasks_used = []
 
@@ -619,14 +601,14 @@
     slab2[me] = two.astype(bf16)
     src2 = lambda c: slab2.at[me]
     start_tasks(tasks, src2, lambda c: slab2.at[c], t2_s, t2_r)
-    turns(5)
+    turns(6)
     wait_tasks(tasks, src2, lambda c: slab2.at[c], t2_s, t2_r)
     three = pack_rows(times(slab2))
     slab3[me] = three.astype(bf16)
     src3 = lambda c: slab3.at[me]
     start_tasks(tasks, src3, lambda c: slab3.at[c], t3_s, t3_r)
     part = -2.4375 * gram + 1.6875 * two - 0.5625 * three
-    turns(5)
+    turns(6)
     wait_tasks(tasks, src3, lambda c: slab3.at[c], t3_s, t3_r)
     final[chip, core] = (part + 0.0625 * pack_rows(times(slab3))).astype(bf16)
 
@@ -654,6 +636,8 @@
 
     turns(2 * chips)
     loop(0, tasks, coef_term)
+    twin = next(wsteps)
+    unpack_to(wall_ref.at[twin], wpacked[twin], rows, width)
     loop(0, tasks, lambda u: swap_part(u).wait())
 
     def add(c):
@@ -665,7 +649,13 @@
             half2[c, p] = pack_pair(one, two).astype(bf16)
 
     loop(0, chips, add)
-    total = ring_reduce(chips, half2, slots2, other, other_in, d_s, d_r, y_sem)
+
+    def advance():
+        for got in wsteps:
+            unpack_to(wall_ref.at[got], wpacked[got], rows, width)
+            break
+
+    total = ring_reduce(chips, half2, slots2, other, other_in, d_s, d_r, y_sem, advance)
     for p in range(pairs):
         for v, piece in enumerate(unpack_pair(total[p], width)):
             mine[2 * p + v] = piece.astype(bf16)
@@ -701,9 +691,9 @@
     loop(0, chips, lambda c: pass_on(c).wait_send())
 
 
-def joint(own, delta, chips, tasks):
-    rows, width = own.shape
-    features = delta.shape[1]
+def joint(delta, sketch, chips, tasks):
+    rows, features = delta.shape
+    width = sketch.shape[0]
     depth = tasks * width // (2 * chips)
     piece = features // (tasks * chips * 2)
     chunk = (tasks // 2, pair_tiles(width), 128)
@@ -715,10 +705,12 @@
         functools.partial(joint_kernel, chips, tasks),
         out_shape=(jax.ShapeDtypeStruct((tasks, chips, 2, piece, width), bf16),
                    jax.ShapeDtypeStruct((tasks, rows, width), bf16)),
-        in_specs=[VMEM, pl.BlockSpec(memory_space=pl.ANY)],
+        in_specs=[pl.BlockSpec(memory_space=pl.ANY)] * 2,
         out_specs=(VMEM, VMEM),
         scratch_shapes=[
-            buf(rows, features), buf(features, rows), buf(tasks, rows, width), buf(tasks, tall, 128),
+            tuple(square_scratch(delta, sketch, chips)),
+            (pltpu.VMEM((rows, width), f32),) + (pltpu.VMEM((width // CB, width, CB), f32),) * 3,
+            buf(features, rows), buf(tasks, rows, width), buf(tasks, tall, 128),
             buf(chips, 2, depth, width), buf(chips, depth, width), buf(chips, high, 128),
             buf(chips, high, 128), buf(chips, 2, high, 128), buf(chips * 2, depth, width),
             buf(chips, 2, high, 128),
@@ -726,14 +718,14 @@
             buf(tasks, chips, 2, piece, width), buf(tasks, chips, piece, width),
             buf(chips, *chunk), buf(chips, *chunk), buf(*chunk), buf(*chunk),
             buf(tasks, piece, width), buf(tasks, piece, width), buf(2, chips, *chunk),
-            buf(tasks, tall, 128), DMA((1,)),
+            buf(tasks, tall, 128),
         ] + pair(tasks) + pair(tasks) + pair(chips) * 3
         + [pltpu.VMEM((depth, width), f32), pltpu.VMEM((rows, width), f32), DMA((4,)), DMA((4,))]
         + pair(chips) * 2
         + pair(tasks) * 5 + pair(chips) * 2 + [DMA((4,))] + pair(tasks) + pair(chips),
         compiler_params=params(2),
         name="joint",
-    )(own, delta)
+    )(delta, sketch)
 
 
 def local(delta, sketch, base):
@@ -741,9 +733,7 @@
     chips = lax.axis_size("row") // 2
     delta_rows, task_sketch = delta[0], sketch[0]
     width = task_sketch.shape[1]
-    sketched, packed = sketch_and_square(delta_rows, task_sketch.T, chips)
-    own = basis_of(packed, sketched, 1.0 / math.sqrt(tasks))
-    coefs, stack = joint(own, delta_rows, chips, tasks)
+    coefs, stack = joint(delta_rows, task_sketch.T, chips, tasks)
     coefs = coefs.reshape(tasks, -1, width)
     update = lax.dot_general(
         stack, coefs, (((0, 2), (0, 2)), ((), ())), preferred_element_type=f32

time: 223 us -> 219 us (0.982)
  Pallas kernels: 217 us -> 213 us
    pallas_call x2 -> x0, Pallas kernels: 44.9 us -> none  [the longest x1 31.4 us: sketch_and_square(): pl.pallas_call(functools.partial(square_kernel, chips), out_shape=(jax.Sh...]
    pallas_call x1, Pallas kernels: 172 us -> 213 us  [joint(): pl.pallas_call(functools.partial(joint_kernel, chips, tasks), out_shape=(...]
where the time goes in v6:
time: 219 us; the launch traced here: 218 us
  Pallas kernels  213 us (97%)
  matrix products  5.11 us (2%)
    pallas_call x1, Pallas kernels, joint(): pl.pallas_call(functools.partial(joint_kernel, chips, tasks), out_shape=(...  213 us
    dot_general x1, matrix products, local(): lax.dot_general(stack, coefs, (((0, 2), (0, 2)), ((), ())), preferred_ele...  5.11 us

profile of v6, /device:TPU:1, one launch (start us, length us, event | category | flops | bytes accessed | tf_op | source)
XLA Modules:
  0.0 218.5 jit_solution(11984913953631720409)
XLA Ops:
  0.0 0.0 copy-start
  0.0 213.4 %joint.1 = (bf16[8,16,2,16,320]{4,3,2,1,0:T(8,128)(2,1)}, bf16[8,448,320]{2,1,0:T(8,128)(2,1)}) custom-call(bf16[448,4096]{1,0:T(8,128)(2,1)} %bitcast.13, bf16[320,4096]{1,0:T(8,128)(2,1)} %bitcast.14), custom_call_target="tpu_custom_call" | custom-call | tf_op jit(solution)/shard_map/joint/pallas_call | solution.py:704
  213.4 0.0 copy-done
  213.4 5.1 %fusion.1 = bf16[448,512]{1,0:T(8,128)(2,1)} fusion(bf16[8,448,320]{2,1,0:T(8,128)(2,1)} %get-tuple-element.7, bf16[8,512,320]{2,1,0:T(8,128)(2,1)} %bitcast.15, bf16[448,512]{1,0:T(8,128)(2,1)S(1)} %copy-done), kind=kOutput, calls=%fused_computation.2 | convolution fusion | flops 1175093248 | bytes 5832704 | tf_op jit(solution)/shard_map/dot_general | solution.py:738
Async XLA Ops:
  0.0 213.4 %copy-start = (bf16[448,512]{1,0:T(8,128)(2,1)S(1)}, bf16[448,512]{1,0:T(8,128)(2,1)}, u32[]{:S(2)}) copy-start(bf16[448,512]{1,0:T(8,128)(2,1)} %param.5) | copy-start | bytes 1376260

commit v7 on v6

--- a/solution.py
+++ b/solution.py
@@ -273,7 +273,7 @@
         top += n - at
     if top < 2 * side:
         term[top:] = jnp.zeros((2 * side - top, 128), f32)
-    turns(4)
+    turns(3)
     barrier_wait(chips, tasks)
 
     def of_side(which):
@@ -284,25 +284,25 @@
 
     swap = remote(term.at[of_side(1 - core)], sib_buf, core_s.at[0], core_r.at[0], {"row": sib})
     swap.start()
-    turns(2)
+    turns(1)
     swap.wait()
     half[...] = term[of_side(core)] + sib_buf[...]
     src, dst = (lambda c: of_chip(half, c)), (lambda d: slots.at[d])
     to_chips(chips, src, dst, a_s, a_r)
-    turns(6)
+    turns(4)
     wait_chips(chips, src, dst, a_s, a_r)
     own = pl.ds(pl.multiple_of(chip * part, part), part)
     total = lax.fori_loop(1, chips, lambda d, t: t + slots[d], half[own])
     out_ref[pl.ds(pl.multiple_of((core * chips + chip) * part, part), part)] = total
     src = lambda c: of_chip(out_ref, core * chips + chip)
     to_chips(chips, src, lambda d: src(0), b_s, b_r)
-    turns(6)
+    turns(4)
     wait_chips(chips, src, lambda d: of_chip(out_ref, core * chips + around(chip, chips - d, chips)),
                b_s, b_r)
     mine, theirs = out_ref.at[of_side(core)], out_ref.at[of_side(1 - core)]
     swap = remote(mine, mine, core_s.at[1], core_r.at[1], {"row": sib})
     swap.start()
-    turns(2)
+    turns(1)
     swap.wait_send()
     remote(mine, theirs, core_s.at[1], core_r.at[1], {"row": sib}).wait_recv()
 
@@ -409,23 +409,39 @@
         return yy * xs + xx % xs
 
     own = at(me)
+    halves = xs == 4
+    across = [d for d in range(1, xs) if d == xs // 2]
+    along = [d for d in range(1, xs) if d != xs // 2]
     send(0, own, name(x, 1 - y))
-    for d in range(1, xs):
+    for d in along if halves else along + across:
         send(d, own, name(x + d, y))
     yield
     twin = at(name(x, 1 - y))
-    across = [d for d in range(1, xs) if d == xs // 2]
-    along = [d for d in range(1, xs) if d != xs // 2]
     arrive(0, twin)
     for d in along:
         send(xs + d, twin, name(x + d, y))
     yield name(x, 1 - y)
+
+    def half(block, which):
+        size = block.shape[0] // 2
+        return block.at[pl.ds(which * size, size)]
+
+    if halves:
+        for d, n, which in ((1, 2, 0), (3, xs, 1)):
+            source = name(x + xs - d, y)
+            arrive(d, at(source))
+            send(n, half(at(source), which), name(x + d, y))
+            yield source
     for d in across:
         block = at(name(x + xs - d, y))
-        arrive(d, block)
+        if halves:
+            arrive(2, half(block, 0))
+            arrive(xs, half(block, 1))
+        else:
+            arrive(d, block)
         send(xs + d, block, name(x, 1 - y))
         yield name(x + xs - d, y)
-    for d in along:
+    for d in [] if halves else along:
         block = name(x + xs - d, y)
         arrive(d, at(block))
         yield block
@@ -462,9 +478,9 @@
 
 
 def joint_kernel(
-    chips, tasks, delta_hbm, sketch_hbm, out_ref, wall_ref, square_refs, basis_refs,
+    chips, tasks, delta_hbm, sketch_hbm, base_ref, merged_ref, out_ref, wall_ref, square_refs, basis_refs,
     turned, stack, packed, terms, sib_buf, half, slots, column, matrix, final,
-    slab, slab2, slab3, parts, sib_parts, half2, slots2, other, other_in, mine, block, gathered, wpacked,
+    slab, slab2, slab3, parts, sib_parts, half2, slots2, other, other_in, mine, block, gathered, acc,
     g_s, g_r, sw_s, sw_r, a_s, a_r, b_s, b_r, c_s, c_r, power, total_w, y1_s, y2_s,
     p_s, p_r, q_s, q_r,
     t1_s, t1_r, t2_s, t2_r, t3_s, t3_r, w_s, w_r, sp_s, sp_r, d_s, d_r, e_s, e_r, y_sem, t4_s, t4_r, f_s, f_r,
@@ -523,6 +539,7 @@
         unpack_to(stack.at[got], packed[got], rows, width)
         ready.append(got)
         gram_term(got, len(ready) - 1)
+        turns(1)
         to_owner(ready[-2], len(ready) - 2)
     to_owner(ready[-1], len(ready) - 1)
     wait_chips(chips, lambda c: half.at[c], lambda d: slots.at[d], a_s, a_r)
@@ -620,8 +637,8 @@
     gather(final, c_s, c_r, y2_s, q_s, q_r, lambda: None, apply)
     weights = total_w[...].astype(bf16)
     wall_ref[me] = weights
-    wpacked[me] = pack_rows(weights)
-    wsteps = spread(tasks, lambda c: wpacked.at[c], w_s, w_r)
+    packed[me] = pack_rows(weights)
+    wsteps = spread(tasks, lambda c: packed.at[c], w_s, w_r)
     next(wsteps)
 
     def swap_part(u):
@@ -637,7 +654,7 @@
     turns(2 * chips)
     loop(0, tasks, coef_term)
     twin = next(wsteps)
-    unpack_to(wall_ref.at[twin], wpacked[twin], rows, width)
+    unpack_to(wall_ref.at[twin], packed[twin], rows, width)
     loop(0, tasks, lambda u: swap_part(u).wait())
 
     def add(c):
@@ -652,7 +669,7 @@
 
     def advance():
         for got in wsteps:
-            unpack_to(wall_ref.at[got], wpacked[got], rows, width)
+            unpack_to(wall_ref.at[got], packed[got], rows, width)
             break
 
     total = ring_reduce(chips, half2, slots2, other, other_in, d_s, d_r, y_sem, advance)
@@ -663,7 +680,7 @@
     tsrc4, tdst4 = (lambda c: mine.at[c]), (lambda c: block.at[c])
     start_tasks(tasks, tsrc4, tdst4, t4_s, t4_r)
     for got in wsteps:
-        unpack_to(wall_ref.at[got], wpacked[got], rows, width)
+        unpack_to(wall_ref.at[got], packed[got], rows, width)
     wait_tasks(tasks, tsrc4, tdst4, t4_s, t4_r)
     for p in range(pairs):
         gathered[core, chip, p] = pack_pair(block[2 * p], block[2 * p + 1])
@@ -690,8 +707,17 @@
         spill(c, 1 - core)
     loop(0, chips, lambda c: pass_on(c).wait_send())
 
-
-def joint(delta, sketch, chips, tasks):
+    def update(t):
+        block = out_ref[t].reshape(acc.shape[1], width)
+        acc[...] += lax.dot_general(wall_ref[t], block, (((1,), (1,)), ((), ())),
+                                    preferred_element_type=f32)
+
+    acc[...] = base_ref[...].astype(f32)
+    loop(0, tasks, update)
+    merged_ref[...] = acc[...].astype(bf16)
+
+
+def joint(delta, sketch, base, chips, tasks):
     rows, features = delta.shape
     width = sketch.shape[0]
     depth = tasks * width // (2 * chips)
@@ -703,11 +729,11 @@
     pair = lambda n: [DMA((n,)), DMA((n,))]
     return pl.pallas_call(
         functools.partial(joint_kernel, chips, tasks),
-        out_shape=(jax.ShapeDtypeStruct((tasks, chips, 2, piece, width), bf16),
-                   jax.ShapeDtypeStruct((tasks, rows, width), bf16)),
-        in_specs=[pl.BlockSpec(memory_space=pl.ANY)] * 2,
-        out_specs=(VMEM, VMEM),
+        out_shape=jax.ShapeDtypeStruct(base.shape, bf16),
+        in_specs=[pl.BlockSpec(memory_space=pl.ANY)] * 2 + [VMEM],
+        out_specs=VMEM,
         scratch_shapes=[
+            buf(tasks, chips, 2, piece, width), buf(tasks, rows, width),
             tuple(square_scratch(delta, sketch, chips)),
             (pltpu.VMEM((rows, width), f32),) + (pltpu.VMEM((width // CB, width, CB), f32),) * 3,
             buf(features, rows), buf(tasks, rows, width), buf(tasks, tall, 128),
@@ -718,27 +744,21 @@
             buf(tasks, chips, 2, piece, width), buf(tasks, chips, piece, width),
             buf(chips, *chunk), buf(chips, *chunk), buf(*chunk), buf(*chunk),
             buf(tasks, piece, width), buf(tasks, piece, width), buf(2, chips, *chunk),
-            buf(tasks, tall, 128),
+            pltpu.VMEM((rows, features // tasks), f32),
         ] + pair(tasks) + pair(tasks) + pair(chips) * 3
         + [pltpu.VMEM((depth, width), f32), pltpu.VMEM((rows, width), f32), DMA((4,)), DMA((4,))]
         + pair(chips) * 2
         + pair(tasks) * 5 + pair(chips) * 2 + [DMA((4,))] + pair(tasks) + pair(chips),
         compiler_params=params(2),
         name="joint",
-    )(delta, sketch)
+    )(delta, sketch, base)
 
 
 def local(delta, sketch, base):
     tasks = lax.axis_size("task")
     chips = lax.axis_size("row") // 2
     delta_rows, task_sketch = delta[0], sketch[0]
-    width = task_sketch.shape[1]
-    coefs, stack = joint(delta_rows, task_sketch.T, chips, tasks)
-    coefs = coefs.reshape(tasks, -1, width)
-    update = lax.dot_general(
-        stack, coefs, (((0, 2), (0, 2)), ((), ())), preferred_element_type=f32
-    )
-    return (base.astype(f32) + update).astype(bf16)
+    return joint(delta_rows, task_sketch.T, base, chips, tasks)
 
 
 def solution(mesh):

time: 219 us -> 223 us (1.018)
  Pallas kernels: 213 us -> 221 us
  matrix products: 5.11 us -> 0 us
    pallas_call x1, Pallas kernels: 213 us -> 221 us  [joint(): pl.pallas_call(functools.partial(joint_kernel, chips, tasks), out_shape=j...]
    dot_general x1 -> x0, matrix products: 5.11 us -> none  [local(): lax.dot_general(stack, coefs, (((0, 2), (0, 2)), ((), ())), preferred_ele...]
where the time goes in v7:
time: 223 us
  Pallas kernels  221 us (99%)
    pallas_call x1, Pallas kernels, joint(): pl.pallas_call(functools.partial(joint_kernel, chips, tasks), out_shape=j...  221 us

profile of v7, /device:TPU:1, one launch (start us, length us, event | category | flops | bytes accessed | tf_op | source)
XLA Modules:
  0.0 222.5 jit_solution(15918187526197771197)
XLA Ops:
  0.0 220.7 %joint.1 = bf16[448,512]{1,0:T(8,128)(2,1)} custom-call(bf16[448,4096]{1,0:T(8,128)(2,1)} %bitcast.4, bf16[320,4096]{1,0:T(8,128)(2,1)} %bitcast.5, bf16[448,512]{1,0:T(8,128)(2,1)} %base_ref.1), custom_call_target="tpu_custom_call" | custom-call | tf_op jit(solution)/shard_map/joint/pallas_call | solution.py:730
  220.7 1.8 copy.5

commit v8 on v7

--- a/solution.py
+++ b/solution.py
@@ -21,7 +21,7 @@
 
 def params(cid):
     return pltpu.CompilerParams(
-        collective_id=cid, has_side_effects=True, vmem_limit_bytes=56 * 1024 * 1024
+        collective_id=cid, has_side_effects=True, vmem_limit_bytes=50 * 1024 * 1024
     )
 
 
@@ -478,10 +478,10 @@
 
 
 def joint_kernel(
-    chips, tasks, delta_hbm, sketch_hbm, base_ref, merged_ref, out_ref, wall_ref, square_refs, basis_refs,
+    chips, tasks, delta_hbm, sketch_hbm, out_ref, wall_ref, square_refs, basis_refs,
     turned, stack, packed, terms, sib_buf, half, slots, column, matrix, final,
-    slab, slab2, slab3, parts, sib_parts, half2, slots2, other, other_in, mine, block, gathered, acc,
-    g_s, g_r, sw_s, sw_r, a_s, a_r, b_s, b_r, c_s, c_r, power, total_w, y1_s, y2_s,
+    slab, slab2, slab3, parts, sib_parts, half2, slots2, other, other_in, mine, block, gathered,
+    g_s, g_r, sw_s, sw_r, a_s, a_r, b_s, b_r, c_s, c_r, power, total_w, gram_other, gram_in, y0_s, y1_s, y2_s,
     p_s, p_r, q_s, q_r,
     t1_s, t1_r, t2_s, t2_r, t3_s, t3_r, w_s, w_r, sp_s, sp_r, d_s, d_r, e_s, e_r, y_sem, t4_s, t4_r, f_s, f_r,
 ):
@@ -519,17 +519,12 @@
         terms[pl.ds(s * (per // 2), per // 2)] = term.reshape(per // 2, 2, depth, width)
         swap_term(s, i).start()
 
-    def to_owner(s, i):
+    def both_cores(s, i):
         swap_term(s, i).wait()
         for e in range(per // 2):
             c = s * (per // 2) + e
             both = terms[c, core].astype(f32) + sib_buf[c].astype(f32)
             half[c] = pack_rows(both).astype(bf16)
-            d = around(c, chips - chip, chips)
-
-            @pl.when(c != chip)
-            def _():
-                remote(half.at[c], slots.at[d], a_s.at[d], a_r.at[d], {"row": c * 2 + core}).start()
 
     steps = spread(tasks, lambda c: packed.at[c], g_s, g_r)
     next(steps)
@@ -540,11 +535,9 @@
         ready.append(got)
         gram_term(got, len(ready) - 1)
         turns(1)
-        to_owner(ready[-2], len(ready) - 2)
-    to_owner(ready[-1], len(ready) - 1)
-    wait_chips(chips, lambda c: half.at[c], lambda d: slots.at[d], a_s, a_r)
-    gram = lax.fori_loop(
-        1, chips, lambda d, t: t + slots[d].astype(f32), half[chip].astype(f32))
+        both_cores(ready[-2], len(ready) - 2)
+    both_cores(ready[-1], len(ready) - 1)
+    gram = ring_reduce(chips, half, slots, gram_other, gram_in, a_s, a_r, y0_s, lambda: None)
     first = gram.astype(bf16)
     slab[me] = first
 
@@ -707,17 +700,8 @@
         spill(c, 1 - core)
     loop(0, chips, lambda c: pass_on(c).wait_send())
 
-    def update(t):
-        block = out_ref[t].reshape(acc.shape[1], width)
-        acc[...] += lax.dot_general(wall_ref[t], block, (((1,), (1,)), ((), ())),
-                                    preferred_element_type=f32)
-
-    acc[...] = base_ref[...].astype(f32)
-    loop(0, tasks, update)
-    merged_ref[...] = acc[...].astype(bf16)
-
-
-def joint(delta, sketch, base, chips, tasks):
+
+def joint(delta, sketch, chips, tasks):
     rows, features = delta.shape
     width = sketch.shape[0]
     depth = tasks * width // (2 * chips)
@@ -729,11 +713,11 @@
     pair = lambda n: [DMA((n,)), DMA((n,))]
     return pl.pallas_call(
         functools.partial(joint_kernel, chips, tasks),
-        out_shape=jax.ShapeDtypeStruct(base.shape, bf16),
-        in_specs=[pl.BlockSpec(memory_space=pl.ANY)] * 2 + [VMEM],
-        out_specs=VMEM,
+        out_shape=(jax.ShapeDtypeStruct((tasks, chips, 2, piece, width), bf16),
+                   jax.ShapeDtypeStruct((tasks, rows, width), bf16)),
+        in_specs=[pl.BlockSpec(memory_space=pl.ANY)] * 2,
+        out_specs=(VMEM, VMEM),
         scratch_shapes=[
-            buf(tasks, chips, 2, piece, width), buf(tasks, rows, width),
             tuple(square_scratch(delta, sketch, chips)),
             (pltpu.VMEM((rows, width), f32),) + (pltpu.VMEM((width // CB, width, CB), f32),) * 3,
             buf(features, rows), buf(tasks, rows, width), buf(tasks, tall, 128),
@@ -744,21 +728,27 @@
             buf(tasks, chips, 2, piece, width), buf(tasks, chips, piece, width),
             buf(chips, *chunk), buf(chips, *chunk), buf(*chunk), buf(*chunk),
             buf(tasks, piece, width), buf(tasks, piece, width), buf(2, chips, *chunk),
-            pltpu.VMEM((rows, features // tasks), f32),
         ] + pair(tasks) + pair(tasks) + pair(chips) * 3
-        + [pltpu.VMEM((depth, width), f32), pltpu.VMEM((rows, width), f32), DMA((4,)), DMA((4,))]
+        + [pltpu.VMEM((depth, width), f32), pltpu.VMEM((rows, width), f32),
+           buf(high, 128), buf(high, 128), DMA((4,)), DMA((4,)), DMA((4,))]
         + pair(chips) * 2
         + pair(tasks) * 5 + pair(chips) * 2 + [DMA((4,))] + pair(tasks) + pair(chips),
         compiler_params=params(2),
         name="joint",
-    )(delta, sketch, base)
+    )(delta, sketch)
 
 
 def local(delta, sketch, base):
     tasks = lax.axis_size("task")
     chips = lax.axis_size("row") // 2
     delta_rows, task_sketch = delta[0], sketch[0]
-    return joint(delta_rows, task_sketch.T, base, chips, tasks)
+    width = task_sketch.shape[1]
+    coefs, stack = joint(delta_rows, task_sketch.T, chips, tasks)
+    coefs = coefs.reshape(tasks, -1, width)
+    update = lax.dot_general(
+        stack, coefs, (((0, 2), (0, 2)), ((), ())), preferred_element_type=f32
+    )
+    return (base.astype(f32) + update).astype(bf16)
 
 
 def solution(mesh):

time: 223 us -> 227 us (1.018)
  matrix products: 0 us -> 5.12 us
    dot_general x0 -> x1, matrix products: none -> 5.12 us  [local(): lax.dot_general(stack, coefs, (((0, 2), (0, 2)), ((), ())), preferred_ele...]
where the time goes in v8:
time: 227 us
  Pallas kernels  220 us (97%)
  matrix products  5.12 us (2%)
    pallas_call x1, Pallas kernels, joint(): pl.pallas_call(functools.partial(joint_kernel, chips, tasks), out_shape=(...  220 us
    dot_general x1, matrix products, local(): lax.dot_general(stack, coefs, (((0, 2), (0, 2)), ((), ())), preferred_ele...  5.12 us

profile of v8, /device:TPU:1, one launch (start us, length us, event | category | flops | bytes accessed | tf_op | source)
XLA Modules:
  0.0 227.0 jit_solution(13886313384027186678)
XLA Ops:
  0.0 0.0 copy-start
  0.0 1.7 copy-done
  1.7 0.0 copy-start.1
  1.7 220.2 %joint.1 = (bf16[8,16,2,16,320]{4,3,2,1,0:T(8,128)(2,1)}, bf16[8,448,320]{2,1,0:T(8,128)(2,1)}) custom-call(bf16[448,4096]{1,0:T(8,128)(2,1)} %bitcast.14, bf16[320,4096]{1,0:T(8,128)(2,1)S(1)} %bitcast.13), custom_call_target="tpu_custom_call" | custom-call | tf_op jit(solution)/shard_map/joint/pallas_call | solution.py:714
  221.9 0.0 copy-done.1
  221.9 5.1 %fusion.1 = bf16[448,512]{1,0:T(8,128)(2,1)} fusion(bf16[8,448,320]{2,1,0:T(8,128)(2,1)} %get-tuple-element.7, bf16[8,512,320]{2,1,0:T(8,128)(2,1)} %bitcast.15, bf16[448,512]{1,0:T(8,128)(2,1)S(1)} %copy-done.1), kind=kOutput, calls=%fused_computation.2 | convolution fusion | flops 1175093248 | bytes 5832704 | tf_op jit(solution)/shard_map/dot_general | solution.py:748
Async XLA Ops:
  0.0 1.7 copy-start
  1.7 220.2 %copy-start.1 = (bf16[448,512]{1,0:T(8,128)(2,1)S(1)}, bf16[448,512]{1,0:T(8,128)(2,1)}, u32[]{:S(2)}) copy-start(bf16[448,512]{1,0:T(8,128)(2,1)} %param.5) | copy-start | bytes 1376260
